TPU v7x, 512 devices: a whole 4x4x16 slice. The times are simulated.
512 devices in a mesh: leaf: 64 (over x, z), front: 8 (over y, core).
Axes of the slice: x: 4, y: 4, z: 16, core: 2. Of those that a mesh axis runs over, the one named last changes fastest.
Arguments:
- added_rows: int32 [30, 8, 1], replicated, may hold values from 0 to 2, as said below
- right_root: float32 [8, 64, 6, 128], P('front', 'leaf'), may hold values from -6 to 6
- right_first: float32 [8, 64, 12, 128], P('front', 'leaf'), may hold values from -6 to 6
- right_second: float32 [8, 64, 24, 128], P('front', 'leaf'), may hold values from -6 to 6
- right_third: float32 [8, 64, 48, 128], P('front', 'leaf'), may hold values from -6 to 6
- right_fourth: float32 [8, 64, 96, 128], P('front', 'leaf'), may hold values from -6 to 6
- inverse_root: bfloat16 [3072, 3072], P('leaf', 'front'), as said below
- inverse_first: bfloat16 [6144, 3072], P('leaf', 'front'), as said below
- inverse_second: bfloat16 [12288, 3072], P('leaf', 'front'), as said below
- inverse_third: bfloat16 [24576, 3072], P('leaf', 'front'), as said below
- inverse_fourth: bfloat16 [49152, 3072], P('leaf', 'front'), as said below
- panel_first: bfloat16 [1024, 6144], P('front', 'leaf'), may hold values from -0.0546875 to 0.0546875
- panel_second: bfloat16 [2048, 12288], P('front', 'leaf'), may hold values from -0.0546875 to 0.0546875
- panel_third: bfloat16 [3072, 24576], P('front', 'leaf'), may hold values from -0.0546875 to 0.0546875
- panel_fourth: bfloat16 [4096, 49152], P('front', 'leaf'), may hold values from -0.0546875 to 0.0546875
Outputs:
- answer_root: float32 [8, 64, 6, 128], P('front', 'leaf')
- answer_first: float32 [8, 64, 12, 128], P('front', 'leaf')
- answer_second: float32 [8, 64, 24, 128], P('front', 'leaf')
- answer_third: float32 [8, 64, 48, 128], P('front', 'leaf')
- answer_fourth: float32 [8, 64, 96, 128], P('front', 'leaf')
Inputs may be any that keep to these rules, and one draw needn't show every extreme that they name: `added_rows`: entries along the last dimension are distinct. `inverse_root`: each node's inverse is lower triangular with a positive diagonal. `inverse_first`: each node's inverse is lower triangular with a positive diagonal. `inverse_second`: each node's inverse is lower triangular with a positive diagonal. `inverse_third`: each node's inverse is lower triangular with a positive diagonal. `inverse_fourth`: each node's inverse is lower triangular with a positive diagonal.
All inputs are finite; a program needn't handle non-finite values.
Results may differ from a plain program's by a relative error of at most 0.0003.
Values sent between devices are 32-bit elements; how exact they have to be, the bound alone decides.
A program may use at most 64 MiB of HBM per device.

v0:
```python
import jax
import jax.numpy as jnp
from jax import lax
from jax.sharding import PartitionSpec as P

B = 128
SB = 24
UBL = 8
LEVELS = 5


exact_mode = lax.Precision.HIGHEST


def swapped(value, axis, apart):
    mask = 2**apart
    pairs = [(source, source ^ mask) for source in range(lax.axis_size(axis))]
    return lax.ppermute(value, axis, pairs)


def group_gather(own_piece, level_index, leaf_pos, leaf_count, wide_top):
    group_size = leaf_count >> level_index
    row_count = own_piece.shape[0]
    owner_node = leaf_pos // group_size
    if level_index <= wide_top:
        whole_axis = lax.all_gather(own_piece, "leaf", axis=0, tiled=True)
        return whole_axis
    current = own_piece
    for bit_index in range(group_size.bit_length() - 1):
        partner = swapped(current, "leaf", bit_index)
        high_side = leaf_pos >> bit_index & 1 == 1
        current = jnp.where(
            high_side,
            jnp.concatenate([partner, current], 0),
            jnp.concatenate([current, partner], 0),
        )
    return current


def group_total(values, level_index, leaf_pos, leaf_count, wide_top):
    group_size = leaf_count >> level_index
    owner_node = leaf_pos // group_size
    if level_index <= wide_top:
        slot_count = 2**level_index
        slot_table = jnp.where(
            jnp.arange(slot_count)[:, None, None] == owner_node,
            values[None],
            jnp.zeros_like(values)[None],
        )
        summed = lax.psum(slot_table, "leaf")
        return summed[owner_node]
    for bit_index in range(group_size.bit_length() - 1):
        values = values + swapped(values, "leaf", bit_index)
    return values


def block_picker(added_rows, level_index, leaf_pos, front_pos, leaf_count, slab_blocks):
    child_size = (leaf_count >> level_index) // 2
    child_node = leaf_pos // child_size
    chosen_ids = added_rows[2 ** (level_index + 1) - 2 + child_node, front_pos]
    return (chosen_ids[:, None] == jnp.arange(slab_blocks)[None, :]).astype(jnp.float32)


def per_device(
    added_rows,
    right_root,
    right_first,
    right_second,
    right_third,
    right_fourth,
    inverse_root,
    inverse_first,
    inverse_second,
    inverse_third,
    inverse_fourth,
    panel_first,
    panel_second,
    panel_third,
    panel_fourth,
):
    rights = (right_root, right_first, right_second, right_third, right_fourth)
    inverses = (inverse_root, inverse_first, inverse_second, inverse_third, inverse_fourth)
    panels = (None, panel_first, panel_second, panel_third, panel_fourth)
    leaf_count = lax.axis_size("leaf")
    front_count = lax.axis_size("front")
    leaf_pos = lax.axis_index("leaf")
    front_pos = lax.axis_index("front")
    wide_top = 0
    slab_blocks = SB // front_count
    pick_count = UBL // front_count
    fresh_rows = pick_count * B
    forward = [None] * LEVELS
    pending = None
    carried = None
    for level_index in reversed(range(LEVELS)):
        group_size = leaf_count >> level_index
        own_piece = rights[level_index][0, 0]
        slab = group_gather(own_piece, level_index, leaf_pos, leaf_count, wide_top)
        if pending is not None:
            fresh = group_total(
                pending[:fresh_rows], level_index + 1, leaf_pos, leaf_count, wide_top
            )
            carried = pending[fresh_rows:]
            one_hot = block_picker(
                added_rows, level_index, leaf_pos, front_pos, leaf_count, slab_blocks
            )
            spread = jnp.einsum(
                "kc,kbr->cbr", one_hot, fresh.reshape(pick_count, B, -1), precision=exact_mode
            )
            spread = spread.reshape(slab_blocks * B, -1)
            spread = spread + swapped(spread, "leaf", (group_size // 2).bit_length() - 1)
            slab = slab - spread
        inverse_tile = inverses[level_index].astype(jnp.float32)
        partial_rows = jnp.dot(
            inverse_tile, slab, precision=exact_mode, preferred_element_type=jnp.float32
        )
        solved = lax.psum(partial_rows, "front")
        forward[level_index] = solved
        if level_index > 0:
            panel_tile = panels[level_index].astype(jnp.float32)
            update = jnp.dot(
                panel_tile, solved, precision=exact_mode, preferred_element_type=jnp.float32
            )
            pending = update if pending is None else update + carried
    answers = [None] * LEVELS
    ancestors = None
    for level_index in range(LEVELS):
        group_size = leaf_count >> level_index
        width_rows = rights[level_index].shape[2]
        target_rows = forward[level_index]
        if level_index > 0:
            panel_tile = panels[level_index].astype(jnp.float32)
            through = lax.dot_general(
                panel_tile,
                ancestors,
                (((0,), (0,)), ((), ())),
                precision=exact_mode,
                preferred_element_type=jnp.float32,
            )
            target_rows = target_rows - lax.psum(through, "front")
        inverse_tile = inverses[level_index].astype(jnp.float32)
        partial_cols = lax.dot_general(
            inverse_tile,
            target_rows,
            (((0,), (0,)), ((), ())),
            precision=exact_mode,
            preferred_element_type=jnp.float32,
        )
        full_slab = group_total(partial_cols, level_index, leaf_pos, leaf_count, wide_top)
        position = leaf_pos % group_size
        own_answer = lax.dynamic_slice_in_dim(full_slab, position * width_rows, width_rows, 0)
        answers[level_index] = own_answer.reshape(1, 1, width_rows, -1)
        if level_index + 1 < LEVELS:
            one_hot = block_picker(
                added_rows, level_index, leaf_pos, front_pos, leaf_count, slab_blocks
            )
            picked = jnp.einsum(
                "kc,cbr->kbr", one_hot, full_slab.reshape(slab_blocks, B, -1), precision=exact_mode
            )
            picked = picked.reshape(pick_count * B, -1)
            ancestors = picked if ancestors is None else jnp.concatenate([picked, ancestors], 0)
    return (answers[0], answers[1], answers[2], answers[3], answers[4])


def solution(mesh):
    in_specs = (
        P(),
        P("front", "leaf", None, None),
        P("front", "leaf", None, None),
        P("front", "leaf", None, None),
        P("front", "leaf", None, None),
        P("front", "leaf", None, None),
        P("leaf", "front"),
        P("leaf", "front"),
        P("leaf", "front"),
        P("leaf", "front"),
        P("leaf", "front"),
        P("front", "leaf"),
        P("front", "leaf"),
        P("front", "leaf"),
        P("front", "leaf"),
    )
    out_specs = (
        P("front", "leaf", None, None),
        P("front", "leaf", None, None),
        P("front", "leaf", None, None),
        P("front", "leaf", None, None),
        P("front", "leaf", None, None),
    )
    return jax.shard_map(
        per_device, mesh=mesh, in_specs=in_specs, out_specs=out_specs, check_vma=False
    )
```

profile of v0, /device:TPU:1, one launch (start us, length us, event | category | flops | bytes accessed | tf_op | source)
XLA Modules:
  0.0 1329.0 jit_solution(17499629452200504914)
XLA Ops:
  7.2 4.5 collective-permute-start.12
  14.3 4.9 collective-permute-start.13
  24.5 3.7 collective-permute-start.9
  29.6 75.8 %all-reduce.8.cloned.1.call-done = f32[768,128]{0,1:T(8,128)} async-done(((f32[768,128]{0,1:T(8,128)}), f32[768,128]{0,1:T(8,128)}) %all-reduce.8.cloned.1.call-update) | async-done | bytes 393232 | tf_op jit(solution)/shard_map/psum | solution.py:117
  112.3 3.6 collective-permute-start.15
  119.1 6.4 collective-permute-start.16
  125.6 4.1 collective-permute-start.11
  129.7 22.5 %collective-permute-done.11 = f32[192,128]{1,0:T(8,128)S(1)} collective-permute-done((f32[192,128]{1,0:T(8,128)S(1)}, f32[192,128]{1,0:T(8,128)S(1)}, u32[]{:S(2)}, u32[]{:S(2)}) %collective-permute-start.11) | collective-permute-done | bytes 98336 | tf_op jit(solution)/shard_map/ppermute | solution.py:18
  156.0 73.5 %all-reduce.10.cloned.1.call-done = f32[384,128]{0,1:T(8,128)} async-done(((f32[384,128]{0,1:T(8,128)}), f32[384,128]{0,1:T(8,128)}) %all-reduce.10.cloned.1.call-update) | async-done | bytes 196624 | tf_op jit(solution)/shard_map/psum | solution.py:117
  233.4 4.2 collective-permute-start.6
  240.3 3.8 collective-permute-done.18
  244.2 7.4 collective-permute-start.19
  254.8 10.1 collective-permute-start.20
  265.0 4.0 collective-permute-start.8
  269.0 17.0 %collective-permute-done.8 = f32[192,128]{1,0:T(8,128)S(1)} collective-permute-done((f32[192,128]{1,0:T(8,128)S(1)}, f32[192,128]{1,0:T(8,128)S(1)}, u32[]{:S(2)}, u32[]{:S(2)}) %collective-permute-start.8) | collective-permute-done | bytes 98336 | tf_op jit(solution)/shard_map/ppermute | solution.py:18
  289.0 77.7 %all-reduce.12.cloned.1.call-done = f32[192,128]{1,0:T(8,128)} async-done(((f32[192,128]{1,0:T(8,128)}), f32[192,128]{1,0:T(8,128)}) %all-reduce.12.cloned.1.call-update) | async-done | bytes 98320 | tf_op jit(solution)/shard_map/psum | solution.py:117
  370.4 4.2 collective-permute-start.1
  376.7 7.4 collective-permute-start.2
  384.1 4.5 collective-permute-start.23
  389.3 3.7 collective-permute-done.23
  393.0 10.8 collective-permute-start.24
  403.8 3.2 collective-permute-start.3
  407.3 3.2 collective-permute-start.25
  410.5 7.9 collective-permute-done.3
  418.4 3.1 collective-permute-start.4
  424.1 26.8 %psum.73 = f32[96,128]{1,0:T(8,128)S(1)} all-reduce(f32[96,128]{1,0:T(8,128)S(1)} %convolution_bitcast_fusion.15), channel_id=1, replica_groups=mesh['leaf'=64,'front'=8] {'front'}, use_global_device_ids=true, to_apply=%region_3.4 | all-reduce | flops 12288 | bytes 98304 | tf_op jit(solution)/shard_map/psum | solution.py:117
  453.1 3.1 collective-permute-done.26
  458.1 4.4 collective-permute-done.27
  462.5 4.8 collective-permute-start.28
  467.3 5.5 collective-permute-done.28
  472.8 4.5 collective-permute-start.29
  477.3 9.3 collective-permute-done.29
  486.6 3.1 collective-permute-start.30
  492.1 4.6 collective-permute-start.31
  497.4 61.7 %all-gather = f32[1,1,384,128]{3,1,0,2:T(1,128)S(1)} all-gather(f32[1,1,6,128]{3,1,0,2:T(1,128)S(1)} %bitcast.157), channel_id=2, replica_groups=mesh['leaf'=64,'front'=8] {'leaf'}, dimensions={2}, use_global_device_ids=true | all-gather | bytes 199680 | tf_op jit(solution)/shard_map/all_gather | solution.py:26
  559.4 47.5 %psum.74 = f32[48,128]{1,0:T(8,128)S(1)} all-reduce(f32[48,128]{1,0:T(8,128)S(1)} %convolution_bitcast_fusion.16), channel_id=1, replica_groups=mesh['leaf'=64,'front'=8] {'front'}, use_global_device_ids=true, to_apply=%region_4.5 | all-reduce | flops 6144 | bytes 49152 | tf_op jit(solution)/shard_map/psum | solution.py:117
  607.9 246.4 %all-reduce.14.cloned.1.call-done = f32[1,384,128]{1,2,0:T(8,128)} async-done(((f32[1,384,128]{1,2,0:T(8,128)}), f32[1,384,128]{1,2,0:T(8,128)}) %all-reduce.14.cloned.1.call-update) | async-done | bytes 196624 | tf_op jit(solution)/shard_map/psum | solution.py:50
  856.7 31.9 %psum.76 = f32[96,128]{1,0:T(8,128)S(1)} all-reduce(f32[96,128]{1,0:T(8,128)S(1)} %convolution_bitcast_fusion.14), channel_id=1, replica_groups=mesh['leaf'=64,'front'=8] {'front'}, use_global_device_ids=true, to_apply=%region_6.7 | all-reduce | flops 12288 | bytes 98304 | tf_op jit(solution)/shard_map/psum | solution.py:140
  891.1 4.1 collective-permute-done.32
  897.8 6.9 collective-permute-done.33
  904.7 4.0 collective-permute-start.34
  908.8 21.9 %collective-permute-done.34 = f32[384,128]{0,1:T(8,128)S(1)} collective-permute-done((f32[384,128]{0,1:T(8,128)S(1)}, f32[384,128]{0,1:T(8,128)S(1)}, u32[]{:S(2)}, u32[]{:S(2)}) %collective-permute-start.34) | collective-permute-done | bytes 196640 | tf_op jit(solution)/shard_map/ppermute | solution.py:18
  930.7 4.5 collective-permute-start.35
  935.2 17.0 %collective-permute-done.35 = f32[384,128]{0,1:T(8,128)S(1)} collective-permute-done((f32[384,128]{0,1:T(8,128)S(1)}, f32[384,128]{0,1:T(8,128)S(1)}, u32[]{:S(2)}, u32[]{:S(2)}) %collective-permute-start.35) | collective-permute-done | bytes 196640 | tf_op jit(solution)/shard_map/ppermute | solution.py:18
  952.3 3.1 collective-permute-start.36
  955.4 4.8 collective-permute-done.36
  962.4 73.8 %all-reduce.16.cloned.1.call-done = f32[192,128]{1,0:T(8,128)} async-done(((f32[192,128]{1,0:T(8,128)}), f32[192,128]{1,0:T(8,128)}) %all-reduce.16.cloned.1.call-update) | async-done | bytes 98320 | tf_op jit(solution)/shard_map/psum | solution.py:140
  1039.8 4.0 collective-permute-done.37
  1043.8 3.4 collective-permute-start.38
  1047.3 6.0 collective-permute-done.38
  1053.3 6.6 collective-permute-start.39
  1059.9 17.6 %collective-permute-done.39 = f32[384,128]{0,1:T(8,128)S(1)} collective-permute-done((f32[384,128]{0,1:T(8,128)S(1)}, f32[384,128]{0,1:T(8,128)S(1)}, u32[]{:S(2)}, u32[]{:S(2)}) %collective-permute-start.39) | collective-permute-done | bytes 196640 | tf_op jit(solution)/shard_map/ppermute | solution.py:18
  1077.6 11.1 collective-permute-start.40
  1088.6 17.7 %collective-permute-done.40 = f32[384,128]{0,1:T(8,128)S(1)} collective-permute-done((f32[384,128]{0,1:T(8,128)S(1)}, f32[384,128]{0,1:T(8,128)S(1)}, u32[]{:S(2)}, u32[]{:S(2)}) %collective-permute-start.40) | collective-permute-done | bytes 196640 | tf_op jit(solution)/shard_map/ppermute | solution.py:18
  1108.8 71.0 %all-reduce.18.cloned.1.call-done = f32[384,128]{0,1:T(8,128)} async-done(((f32[384,128]{0,1:T(8,128)}), f32[384,128]{0,1:T(8,128)}) %all-reduce.18.cloned.1.call-update) | async-done | bytes 196624 | tf_op jit(solution)/shard_map/psum | solution.py:140
  1183.7 3.9 collective-permute-done.41
  1187.6 3.5 collective-permute-start.42
  1191.1 6.6 collective-permute-done.42
  1197.7 6.0 collective-permute-start.43
  1203.7 18.3 %collective-permute-done.43 = f32[384,128]{0,1:T(8,128)S(1)} collective-permute-done((f32[384,128]{0,1:T(8,128)S(1)}, f32[384,128]{0,1:T(8,128)S(1)}, u32[]{:S(2)}, u32[]{:S(2)}) %collective-permute-start.43) | collective-permute-done | bytes 196640 | tf_op jit(solution)/shard_map/ppermute | solution.py:18
  1224.7 78.7 %all-reduce.20.cloned.1.call-done = f32[768,128]{0,1:T(8,128)} async-done(((f32[768,128]{0,1:T(8,128)}), f32[768,128]{0,1:T(8,128)}) %all-reduce.20.cloned.1.call-update) | async-done | bytes 393232 | tf_op jit(solution)/shard_map/psum | solution.py:140
  1304.9 2.6 collective-permute-start.44
  1311.3 3.6 collective-permute-start.45
  1316.5 4.9 collective-permute-done.45
  (177 shorter events, 83.2 us)
Async XLA Ops:
  7.2 98.2 %copy-start = (bf16[512,768]{1,0:T(8,128)(2,1)S(1)}, bf16[512,768]{1,0:T(8,128)(2,1)}, u32[]{:S(2)}) copy-start(bf16[512,768]{1,0:T(8,128)(2,1)} %param.29) | copy-start | bytes 2359300
  7.2 98.1 %all-reduce.8.cloned.1.call-start = ((), (), s32[]{:S(2)}) async-start(), calls=%async_computation | async-start | bytes 786432 | tf_op jit(solution)/shard_map/psum | solution.py:117
  7.2 6.2 collective-permute-start.12
  14.3 6.9 collective-permute-start.13
  23.8 205.7 %all-reduce.10.cloned.1.call-start = ((), (), s32[]{:S(2)}) async-start(), calls=%async_computation.1 | async-start | bytes 393216 | tf_op jit(solution)/shard_map/psum | solution.py:117
  24.5 91.4 %collective-permute-start.9 = (f32[48,128]{1,0:T(8,128)S(1)}, f32[48,128]{1,0:T(8,128)S(1)}, u32[]{:S(2)}, u32[]{:S(2)}) collective-permute-start(f32[48,128]{1,0:T(8,128)S(1)} %bitcast.151), channel_id=1, source_target_pairs={{0,8},{8,0},{16,24},{24,16},{32,40},{40,32},{48,56},{56,48},{64,72... | collective-permute-start | bytes 73736 | tf_op jit(solution)/shard_map/ppermute | solution.py:18
  107.2 5.0 collective-permute-start.14
  112.3 6.6 collective-permute-start.15
  115.9 9.6 collective-permute-start.10
  118.9 33.3 %copy-start.4 = (bf16[384,384]{1,0:T(8,128)(2,1)S(1)}, bf16[384,384]{1,0:T(8,128)(2,1)}, u32[]{:S(2)}) copy-start(bf16[384,384]{1,0:T(8,128)(2,1)} %param.24) | copy-start | bytes 884740
  119.1 33.1 %collective-permute-start.16 = (f32[384,128]{1,0:T(8,128)S(1)}, f32[384,128]{1,0:T(8,128)S(1)}, u32[]{:S(2)}, u32[]{:S(2)}) collective-permute-start(f32[384,128]{1,0:T(8,128)S(1)} %bitcast.141), channel_id=1, source_target_pairs={{0,32},{8,40},{16,48},{24,56},{32,0},{40,8},{48,16},{56,24},{64,96... | collective-permute-start | bytes 589832 | tf_op jit(solution)/shard_map/ppermute | solution.py:18
  125.6 26.6 %collective-permute-start.11 = (f32[192,128]{1,0:T(8,128)S(1)}, f32[192,128]{1,0:T(8,128)S(1)}, u32[]{:S(2)}, u32[]{:S(2)}) collective-permute-start(f32[192,128]{1,0:T(8,128)S(1)} %maximum_select_fusion.7), channel_id=1, source_target_pairs={{0,32},{8,40},{16,48},{24,56},{32,0},{40,8},{48,16},{56,24},{64,96... | collective-permute-start | bytes 294920 | tf_op jit(solution)/shard_map/ppermute | solution.py:18
  152.2 77.3 %copy-start.3 = (bf16[384,384]{1,0:T(8,128)(2,1)S(1)}, bf16[384,384]{1,0:T(8,128)(2,1)}, u32[]{:S(2)}) copy-start(bf16[384,384]{1,0:T(8,128)(2,1)} %param.28) | copy-start | bytes 884740
  153.4 213.3 %all-reduce.12.cloned.1.call-start = ((), (), s32[]{:S(2)}) async-start(), calls=%async_computation.2 | async-start | bytes 196608 | tf_op jit(solution)/shard_map/psum | solution.py:117
  154.1 79.3 %collective-permute-start.5 = (f32[24,128]{1,0:T(8,128)S(1)}, f32[24,128]{1,0:T(8,128)S(1)}, u32[]{:S(2)}, u32[]{:S(2)}) collective-permute-start(f32[24,128]{1,0:T(8,128)S(1)} %bitcast.155), channel_id=1, source_target_pairs={{0,8},{8,0},{16,24},{24,16},{32,40},{40,32},{48,56},{56,48},{64,72... | collective-permute-start | bytes 36872 | tf_op jit(solution)/shard_map/ppermute | solution.py:18
  230.9 6.8 collective-permute-start.17
  233.4 18.1 %collective-permute-start.6 = (f32[48,128]{1,0:T(8,128)S(1)}, f32[48,128]{1,0:T(8,128)S(1)}, u32[]{:S(2)}, u32[]{:S(2)}) collective-permute-start(f32[48,128]{1,0:T(8,128)S(1)} %maximum_select_fusion.13), channel_id=1, source_target_pairs={{0,16},{8,24},{16,0},{24,8},{32,48},{40,56},{48,32},{56,40},{64,80... | collective-permute-start | bytes 73736 | tf_op jit(solution)/shard_map/ppermute | solution.py:18
  237.6 6.5 collective-permute-start.18
  244.2 10.5 collective-permute-start.19
  251.6 13.4 %collective-permute-start.7 = (f32[96,128]{1,0:T(8,128)S(1)}, f32[96,128]{1,0:T(8,128)S(1)}, u32[]{:S(2)}, u32[]{:S(2)}) collective-permute-start(f32[96,128]{1,0:T(8,128)S(1)} %maximum_select_fusion.10), channel_id=1, source_target_pairs={{0,32},{8,40},{16,48},{24,56},{32,0},{40,8},{48,16},{56,24},{64,96... | collective-permute-start | bytes 147464 | tf_op jit(solution)/shard_map/ppermute | solution.py:18
  254.8 31.2 %copy-start.6 = (bf16[192,384]{1,0:T(8,128)(2,1)S(1)}, bf16[192,384]{1,0:T(8,128)(2,1)}, u32[]{:S(2)}) copy-start(bf16[192,384]{1,0:T(8,128)(2,1)} %param.23) | copy-start | bytes 442372
  254.8 31.2 %collective-permute-start.20 = (f32[384,128]{1,0:T(8,128)S(1)}, f32[384,128]{1,0:T(8,128)S(1)}, u32[]{:S(2)}, u32[]{:S(2)}) collective-permute-start(f32[384,128]{1,0:T(8,128)S(1)} %bitcast.139), channel_id=1, source_target_pairs={{0,64},{8,72},{16,80},{24,88},{32,96},{40,104},{48,112},{56,120},{... | collective-permute-start | bytes 589832 | tf_op jit(solution)/shard_map/ppermute | solution.py:18
  265.0 21.0 %collective-permute-start.8 = (f32[192,128]{1,0:T(8,128)S(1)}, f32[192,128]{1,0:T(8,128)S(1)}, u32[]{:S(2)}, u32[]{:S(2)}) collective-permute-start(f32[192,128]{1,0:T(8,128)S(1)} %maximum_select_fusion.6), channel_id=1, source_target_pairs={{0,64},{8,72},{16,80},{24,88},{32,96},{40,104},{48,112},{56,120},{... | collective-permute-start | bytes 294920 | tf_op jit(solution)/shard_map/ppermute | solution.py:18
  287.0 79.7 %copy-start.7 = (bf16[256,192]{0,1:T(8,128)(2,1)S(1)}, bf16[256,192]{0,1:T(8,128)(2,1)}, u32[]{:S(2)}) copy-start(bf16[256,192]{0,1:T(8,128)(2,1)} %param.27) | copy-start | bytes 294916
  287.0 567.3 %all-reduce.14.cloned.1.call-start = ((), (), s32[]{:S(2)}) async-start(), calls=%async_computation.3 | async-start | bytes 393216 | tf_op jit(solution)/shard_map/psum | solution.py:50
  287.1 83.3 %collective-permute-start = (f32[12,128]{1,0:T(8,128)S(1)}, f32[12,128]{1,0:T(8,128)S(1)}, u32[]{:S(2)}, u32[]{:S(2)}) collective-permute-start(f32[12,128]{1,0:T(8,128)S(1)} %bitcast.149), channel_id=1, source_target_pairs={{0,8},{8,0},{16,24},{24,16},{32,40},{40,32},{48,56},{56,48},{64,72... | collective-permute-start | bytes 18440 | tf_op jit(solution)/shard_map/ppermute | solution.py:18
  367.9 6.7 collective-permute-start.21
  370.4 6.2 collective-permute-start.1
  374.6 9.4 collective-permute-start.22
  376.7 27.1 %collective-permute-start.2 = (f32[48,128]{1,0:T(8,128)S(1)}, f32[48,128]{1,0:T(8,128)S(1)}, u32[]{:S(2)}, u32[]{:S(2)}) collective-permute-start(f32[48,128]{1,0:T(8,128)S(1)} %maximum_select_fusion.12), channel_id=1, source_target_pairs={{0,32},{8,40},{16,48},{24,56},{32,0},{40,8},{48,16},{56,24},{64,96... | collective-permute-start | bytes 73736 | tf_op jit(solution)/shard_map/ppermute | solution.py:18
  384.1 8.9 collective-permute-start.23
  393.0 14.0 %collective-permute-start.24 = (f32[128,128]{0,1:T(8,128)S(1)}, f32[128,128]{0,1:T(8,128)S(1)}, u32[]{:S(2)}, u32[]{:S(2)}) collective-permute-start(f32[128,128]{0,1:T(8,128)S(1)} %add.225), channel_id=1, source_target_pairs={{0,64},{8,72},{16,80},{24,88},{32,96},{40,104},{48,112},{56,120},{... | collective-permute-start | bytes 196616 | tf_op jit(solution)/shard_map/ppermute | solution.py:18
  403.8 14.6 %collective-permute-start.3 = (f32[96,128]{1,0:T(8,128)S(1)}, f32[96,128]{1,0:T(8,128)S(1)}, u32[]{:S(2)}, u32[]{:S(2)}) collective-permute-start(f32[96,128]{1,0:T(8,128)S(1)} %maximum_select_fusion.9), channel_id=1, source_target_pairs={{0,64},{8,72},{16,80},{24,88},{32,96},{40,104},{48,112},{56,120},{... | collective-permute-start | bytes 147464 | tf_op jit(solution)/shard_map/ppermute | solution.py:18
  407.3 16.5 %collective-permute-start.25 = (f32[384,128]{1,0:T(8,128)S(1)}, f32[384,128]{1,0:T(8,128)S(1)}, u32[]{:S(2)}, u32[]{:S(2)}) collective-permute-start(f32[384,128]{1,0:T(8,128)S(1)} %bitcast.137), channel_id=1, source_target_pairs={{0,128},{8,136},{16,144},{24,152},{32,160},{40,168},{48,176},{56,1... | collective-permute-start | bytes 589832 | tf_op jit(solution)/shard_map/ppermute | solution.py:18
  418.4 5.4 collective-permute-start.4
  424.0 26.8 %copy-start.11 = (bf16[128,96]{0,1:T(8,128)(2,1)S(1)}, bf16[128,96]{0,1:T(8,128)(2,1)}, u32[]{:S(2)}) copy-start(bf16[128,96]{0,1:T(8,128)(2,1)} %param.26) | copy-start | bytes 73732
  451.1 5.0 collective-permute-start.26
  456.2 6.3 collective-permute-start.27
  462.5 10.3 collective-permute-start.28
  472.8 13.7 %collective-permute-start.29 = (f32[128,128]{0,1:T(8,128)S(1)}, f32[128,128]{0,1:T(8,128)S(1)}, u32[]{:S(2)}, u32[]{:S(2)}) collective-permute-start(f32[128,128]{0,1:T(8,128)S(1)} %add.231), channel_id=1, source_target_pairs={{0,64},{8,72},{16,80},{24,88},{32,96},{40,104},{48,112},{56,120},{... | collective-permute-start | bytes 196616 | tf_op jit(solution)/shard_map/ppermute | solution.py:18
  486.6 5.3 collective-permute-start.30
  492.1 67.0 %collective-permute-start.31 = (f32[384,128]{1,0:T(8,128)S(1)}, f32[384,128]{1,0:T(8,128)S(1)}, u32[]{:S(2)}, u32[]{:S(2)}) collective-permute-start(f32[384,128]{1,0:T(8,128)S(1)} %bitcast.135), channel_id=1, source_target_pairs={{0,256},{8,264},{16,272},{24,280},{32,288},{40,296},{48,304},{56,3... | collective-permute-start | bytes 589832 | tf_op jit(solution)/shard_map/ppermute | solution.py:18
  497.4 61.7 %copy-start.10 = (bf16[48,384]{1,0:T(8,128)(2,1)S(1)}, bf16[48,384]{1,0:T(8,128)(2,1)}, u32[]{:S(2)}) copy-start(bf16[48,384]{1,0:T(8,128)(2,1)} %param.21) | copy-start | bytes 110596
  607.9 428.3 %all-reduce.16.cloned.1.call-start = ((), (), s32[]{:S(2)}) async-start(), calls=%async_computation.4 | async-start | bytes 196608 | tf_op jit(solution)/shard_map/psum | solution.py:140
  888.9 6.4 collective-permute-start.32
  895.3 9.4 collective-permute-start.33
  904.7 26.0 %collective-permute-start.34 = (f32[384,128]{0,1:T(8,128)S(1)}, f32[384,128]{0,1:T(8,128)S(1)}, u32[]{:S(2)}, u32[]{:S(2)}) collective-permute-start(f32[384,128]{0,1:T(8,128)S(1)} %add.238), channel_id=1, source_target_pairs={{0,32},{8,40},{16,48},{24,56},{32,0},{40,8},{48,16},{56,24},{64,96... | collective-permute-start | bytes 589832 | tf_op jit(solution)/shard_map/ppermute | solution.py:18
  930.7 21.5 %collective-permute-start.35 = (f32[384,128]{0,1:T(8,128)S(1)}, f32[384,128]{0,1:T(8,128)S(1)}, u32[]{:S(2)}, u32[]{:S(2)}) collective-permute-start(f32[384,128]{0,1:T(8,128)S(1)} %add.239), channel_id=1, source_target_pairs={{0,64},{8,72},{16,80},{24,88},{32,96},{40,104},{48,112},{56,120},{... | collective-permute-start | bytes 589832 | tf_op jit(solution)/shard_map/ppermute | solution.py:18
  952.3 7.9 collective-permute-start.36
  962.3 73.9 %copy-start.8 = (f32[192,128]{1,0:T(8,128)S(1)}, f32[192,128]{1,0:T(8,128)}, u32[]{:S(2)}) copy-start(f32[192,128]{1,0:T(8,128)} %all-reduce.12.cloned.1.call-done) | copy-start | bytes 294916
  962.3 217.5 %all-reduce.18.cloned.1.call-start = ((), (), s32[]{:S(2)}) async-start(), calls=%async_computation.5 | async-start | bytes 393216 | tf_op jit(solution)/shard_map/psum | solution.py:140
  1037.4 6.4 collective-permute-start.37
  1043.8 9.4 collective-permute-start.38
  1053.3 24.2 %collective-permute-start.39 = (f32[384,128]{0,1:T(8,128)S(1)}, f32[384,128]{0,1:T(8,128)S(1)}, u32[]{:S(2)}, u32[]{:S(2)}) collective-permute-start(f32[384,128]{0,1:T(8,128)S(1)} %add.245), channel_id=1, source_target_pairs={{0,32},{8,40},{16,48},{24,56},{32,0},{40,8},{48,16},{56,24},{64,96... | collective-permute-start | bytes 589832 | tf_op jit(solution)/shard_map/ppermute | solution.py:18
  1077.6 28.8 %collective-permute-start.40 = (f32[384,128]{0,1:T(8,128)S(1)}, f32[384,128]{0,1:T(8,128)S(1)}, u32[]{:S(2)}, u32[]{:S(2)}) collective-permute-start(f32[384,128]{0,1:T(8,128)S(1)} %add.246), channel_id=1, source_target_pairs={{0,64},{8,72},{16,80},{24,88},{32,96},{40,104},{48,112},{56,120},{... | collective-permute-start | bytes 589832 | tf_op jit(solution)/shard_map/ppermute | solution.py:18
  1108.8 71.1 %copy-start.5 = (f32[384,128]{0,1:T(8,128)S(1)}, f32[384,128]{0,1:T(8,128)}, u32[]{:S(2)}) copy-start(f32[384,128]{0,1:T(8,128)} %all-reduce.10.cloned.1.call-done) | copy-start | bytes 589828
  1108.8 194.6 %all-reduce.20.cloned.1.call-start = ((), (), s32[]{:S(2)}) async-start(), calls=%async_computation.6 | async-start | bytes 786432 | tf_op jit(solution)/shard_map/psum | solution.py:140
  1181.1 6.4 collective-permute-start.41
  1187.6 10.1 collective-permute-start.42
  1197.7 24.3 %collective-permute-start.43 = (f32[384,128]{0,1:T(8,128)S(1)}, f32[384,128]{0,1:T(8,128)S(1)}, u32[]{:S(2)}, u32[]{:S(2)}) collective-permute-start(f32[384,128]{0,1:T(8,128)S(1)} %add.251), channel_id=1, source_target_pairs={{0,32},{8,40},{16,48},{24,56},{32,0},{40,8},{48,16},{56,24},{64,96... | collective-permute-start | bytes 589832 | tf_op jit(solution)/shard_map/ppermute | solution.py:18
  1223.3 80.1 %copy-start.1 = (bf16[768,384]{1,0:T(8,128)(2,1)S(1)}, bf16[768,384]{1,0:T(8,128)(2,1)}, u32[]{:S(2)}) copy-start(bf16[768,384]{1,0:T(8,128)(2,1)} %param.25) | copy-start | bytes 1769476
  1224.6 78.8 %copy-start.2 = (f32[768,128]{0,1:T(8,128)S(1)}, f32[768,128]{0,1:T(8,128)}, u32[]{:S(2)}) copy-start(f32[768,128]{0,1:T(8,128)} %all-reduce.8.cloned.1.call-done) | copy-start | bytes 1179652
  1304.9 6.4 collective-permute-start.44
  1311.3 10.1 collective-permute-start.45
  (6 other events, 20.4 us)
Sparse Core Ops, SparseCore 0:
  23.9 81.3 all-reduce.7
  153.5 75.9 all-reduce.9
  287.1 79.5 all-reduce.11
  608.0 246.2 all-reduce.13
  962.5 73.6 all-reduce.15
  1108.9 70.9 all-reduce.17
  1224.7 78.6 all-reduce.19
where the time goes:
time: 1340 us; the launch traced here: 1330 us
  waiting for transfers between devices  920 us (69%)
  starting transfers between devices  189 us (14%)
  blocking collectives  168 us (13%)
  matrix products  22.9 us (2%)
  between operations  15.4 us (1%)
    psum x1, waiting for transfers between devices, group_total(): summed = lax.psum(slot_table, 'leaf')  246 us
    psum x3, waiting for transfers between devices, per_device(): solved = lax.psum(partial_rows, 'front')  227 us
    psum x3, waiting for transfers between devices, per_device(): target_rows = target_rows - lax.psum(through, 'front')  224 us
    ppermute x46, waiting for transfers between devices, swapped(): return lax.ppermute(value, axis, pairs)  223 us
    ppermute x46, starting transfers between devices, swapped(): return lax.ppermute(value, axis, pairs)  188 us
    psum x2, blocking collectives, per_device(): solved = lax.psum(partial_rows, 'front')  74.4 us
    all_gather x1, blocking collectives, group_gather(): whole_axis = lax.all_gather(own_piece, 'leaf', axis=0, tiled=True)  61.7 us
    psum x1, blocking collectives, per_device(): target_rows = target_rows - lax.psum(through, 'front')  31.9 us
  transfers between devices with their start and end apart: 53, of which 37 were waited for; matrix products, arithmetic and copies ran while one was open for 1% of the time, Pallas kernels for 0%

commit v1 on v0

v1 whole, which is shorter than its diff:
```python
import jax
import jax.numpy as jnp
from jax import lax
from jax.experimental import pallas as pl
from jax.experimental.pallas import tpu as pltpu
from jax.sharding import PartitionSpec as P

MESH = pl.DeviceIdType.MESH
B = 128
LEVELS = 5
NZ = 16
NX = 4
NY = 4
SLAB = 384
ROWS = (48, 96, 192, 384, 768)
OWN = (6, 12, 24, 48, 96)

SCRATCH = {
    "bx0": (4, 6, 128), "bx1": (2, 12, 128),
    "b0": (16, 4, 6, 128), "b1": (16, 2, 12, 128), "b2": (SLAB, 128), "b3": (SLAB, 128), "c4": (SLAB, 128),
    "c3": (SLAB, 128), "c2": (SLAB, 128), "c1": (SLAB, 128), "c0": (SLAB, 128),
    "u4": (512, 128), "u3": (384, 128), "u2": (256, 128), "u1": (128, 128),
    "ur4": (4, 32, 128), "us4": (32, 128), "ug4": (256, 128),
    "ur3": (8, 16, 128), "us3": (16, 128), "ug3": (256, 128),
    "ur2": (16, 8, 128), "us2": (2, 8, 128), "ug2": (16, 2, 8, 128),
    "ur1": (16, 8, 128), "ux1": (4, 8, 128), "uo1": (8, 128), "us1": (2, 8, 128), "ug1": (16, 2, 8, 128),
    "s0": (SLAB, 128), "s1": (SLAB, 128), "s2": (SLAB, 128), "s3": (SLAB, 128), "s4": (SLAB, 128),
    "k0": (16, 2, 8, 128), "kr0": (16, 2, 8, 128), "kx0": (2, 8, 128), "kt0": (4, 8, 128), "ks0": (8, 128), "z0": (16, 8, 128),
    "k1": (16, 2, 8, 128), "kr1": (16, 2, 8, 128), "kx1": (2, 8, 128), "kt1": (8, 128), "ks1": (8, 128), "z1": (16, 8, 128),
    "k2": (256, 128), "kr2": (16, 16, 128), "ks2": (16, 128), "z2": (128, 128),
    "k3": (256, 128), "kr3": (8, 32, 128), "ks3": (32, 128), "z3": (128, 128),
    "ar4": (4, 96, 128), "ar3": (8, 48, 128), "ar2": (16, 24, 128),
    "ax1": (192, 128), "am1": (192, 128), "ap1": (16, 12, 128), "ar1": (16, 12, 128),
    "ax0": (4, 96, 128), "am0": (96, 128), "ap0": (16, 6, 128), "ar0": (16, 6, 128),
}
for _way in "fb":
    for _l in range(LEVELS):
        _h = ROWS[_l] // 2
        SCRATCH[f"{_way}p{_l}"] = (2 * _h, 128)
        SCRATCH[f"{_way}c{_l}"] = (_h, 128)
        SCRATCH[f"{_way}h{_l}"] = (_h, 128)
        if _l >= 3:
            SCRATCH[f"{_way}r{_l}"] = (4, _h // 4, 128)
            SCRATCH[f"{_way}q{_l}"] = (_h // 4, 128)
            SCRATCH[f"{_way}g{_l}"] = (_h, 128)
        else:
            SCRATCH[f"{_way}r{_l}"] = (4, _h, 128)
            SCRATCH[f"{_way}g{_l}"] = (_h, 128)
        SCRATCH[f"{_way}y{_l}"] = (2 * _h, 128)
NAMES = tuple(SCRATCH)
SEMS = 128


def split(values):
    high = values.astype(jnp.bfloat16)
    low = (values - high.astype(jnp.float32)).astype(jnp.bfloat16)
    return jnp.concatenate([high, low], axis=1)


def times(matrix, values):
    both = jnp.dot(matrix, split(values), preferred_element_type=jnp.float32)
    return both[:, :128] + both[:, 128:]


def transposed_times(matrix, values):
    both = lax.dot_general(
        matrix, split(values), (((0,), (0,)), ((), ())), preferred_element_type=jnp.float32
    )
    return both[:, :128] + both[:, 128:]


def rows_of(index, count):
    return pl.ds(pl.multiple_of(index * count, 8), count)


def total(ref):
    parts = [ref[j] for j in range(ref.shape[0])]
    while len(parts) > 1:
        parts = [parts[j] + parts[j + 1] for j in range(0, len(parts), 2)]
    return parts[0]


def kernel(added, *refs):
    rights, refs = refs[:5], refs[5:]
    inverses, refs = refs[:5], refs[5:]
    panels, refs = (None,) + refs[:4], refs[4:]
    outs, refs = refs[:5], refs[5:]
    v = dict(zip(NAMES, refs[: len(NAMES)]))
    send_sems, recv_sems = refs[len(NAMES) :]

    leaf = lax.axis_index("leaf")
    front = lax.axis_index("front")
    x, z = leaf // NZ, leaf % NZ
    y, core = front // 2, front % 2
    pair = x % 2

    counter = [0]
    sent = []

    def at_z(n, i):
        d = n // 2 + (i + 1) // 2 * (1 - 2 * (i % 2))
        there = (z % n + d) % n
        return there, (x * NZ + z - z % n + there, front)

    def at_x(d):
        other = (x + d) % NX
        return other, (other * NZ + z, front)

    x_mate = ((x + 1 - 2 * pair) * NZ + z, front)
    core_mate = (leaf, front + 1 - 2 * core)

    def at_y(d):
        other = (y + d) % NY
        return other, (leaf, other * 2 + core)

    def begin():
        counter[0] += 1
        return counter[0] - 1

    def send(src, dst, k, device):
        pltpu.make_async_remote_copy(
            src_ref=src, dst_ref=dst, send_sem=send_sems.at[k], recv_sem=recv_sems.at[k],
            device_id=device, device_id_type=MESH,
        ).start()

    def await_bytes(like, k, sems):
        pltpu.make_async_copy(like, like, sems.at[k]).wait()

    def scatter_z(n, src, rows, dst):
        k = begin()
        whole_pieces = len(src.shape) > 2

        def piece(i):
            return src.at[i] if whole_pieces else src.at[rows_of(i, rows)]

        def step(i, _):
            there, device = at_z(n, i)
            send(piece(there), dst.at[z % n], k, device)
            return 0

        lax.fori_loop(0, n - 1, step, 0)
        here = z % n
        dst[here] = src[here] if whole_pieces else src[rows_of(here, rows), :]
        like = dst.at[pl.ds(0, n - 1)]
        sent.append((like, k))
        return lambda: await_bytes(like, k, recv_sems)

    def gather_z(n, src, rows, dst):
        k = begin()
        whole_pieces = len(dst.shape) > 2
        here = z % n
        spot = dst.at[here] if whole_pieces else dst.at[rows_of(here, rows)]

        def step(i, _):
            _, device = at_z(n, i)
            send(src, spot, k, device)
            return 0

        lax.fori_loop(0, n - 1, step, 0)
        if whole_pieces:
            dst[here] = src[...]
        else:
            dst[rows_of(here, rows), :] = src[...]
        like = dst.at[pl.ds(0, (n - 1) if whole_pieces else (n - 1) * rows)]
        sent.append((like, k))
        return lambda: await_bytes(like, k, recv_sems)

    def to_one(src, dst, device):
        k = begin()
        send(src, dst, k, device)
        sent.append((dst, k))
        return lambda: await_bytes(dst, k, recv_sems)

    def to_x(pieces, dst):
        k = begin()
        for d in (2, 1, 3):
            other, device = at_x(d)
            send(pieces(other), dst.at[x], k, device)
        like = dst.at[pl.ds(0, 3)]
        sent.append((like, k))
        return lambda: await_bytes(like, k, recv_sems)

    def to_y(pieces, spot, like):
        k = begin()
        for d in (2, 1, 3):
            other, device = at_y(d)
            send(pieces(other), spot, k, device)
        sent.append((like, k))
        return lambda: await_bytes(like, k, recv_sems)

    def front_sum(way, level, meanwhile=None):
        term, from_core, half = v[f"{way}p{level}"], v[f"{way}c{level}"], v[f"{way}h{level}"]
        received, summed, whole = v[f"{way}r{level}"], v[f"{way}g{level}"], v[f"{way}y{level}"]
        h = ROWS[level] // 2
        done = to_one(term.at[rows_of(1 - core, h)], from_core, core_mate)
        done()
        half[...] = term[rows_of(core, h), :] + from_core[...]
        if level >= 3:
            q = h // 4
            piece = v[f"{way}q{level}"]
            done = to_y(lambda other: half.at[rows_of(other, q)], received.at[y], received.at[pl.ds(0, 3)])
            received[y] = half[rows_of(y, q), :]
            if meanwhile is not None:
                meanwhile()
            done()
            piece[...] = total(received)
            done = to_y(lambda other: piece, summed.at[rows_of(y, q)], summed.at[pl.ds(0, 3 * q)])
            summed[rows_of(y, q), :] = piece[...]
            done()
        else:
            done = to_y(lambda other: half, received.at[y], received.at[pl.ds(0, 3)])
            received[y] = half[...]
            if meanwhile is not None:
                meanwhile()
            done()
            summed[...] = total(received)
        done = to_one(summed, whole.at[rows_of(core, h)], core_mate)
        whole[rows_of(core, h), :] = summed[...]
        done()
        return whole

    def choice(level, child):
        block = added[2 ** (level + 1) - 2 + child, front, 0]
        return [jnp.where(block == j, 1.0, 0.0).astype(jnp.float32) for j in range(3)]

    def choices(level):
        node = leaf // (64 >> level)
        return choice(level, 2 * node), choice(level, 2 * node + 1)

    def place(level, b, low, high):
        to_low, to_high = choices(level)
        target = v[f"c{level}"]
        for j in range(3):
            spot = slice(j * B, (j + 1) * B)
            target[spot, :] = b[spot, :] - low * to_low[j] - high * to_high[j]

    def pick(s, weights):
        return s[0:B, :] * weights[0] + s[B : 2 * B, :] * weights[1] + s[2 * B :, :] * weights[2]

    barrier = pltpu.get_barrier_semaphore()

    def greet(i, _):
        _, device = at_z(NZ, i)
        pl.semaphore_signal(barrier, inc=1, device_id=device, device_id_type=MESH)
        return 0

    lax.fori_loop(0, NZ - 1, greet, 0)
    for d in (1, 2, 3):
        pl.semaphore_signal(barrier, inc=1, device_id=at_x(d)[1], device_id_type=MESH)
        pl.semaphore_signal(barrier, inc=1, device_id=at_y(d)[1], device_id_type=MESH)
    pl.semaphore_signal(barrier, inc=1, device_id=core_mate, device_id_type=MESH)
    pl.semaphore_wait(barrier, NZ - 1 + 7)

    done_b4 = gather_z(4, rights[4].at[0, 0], 96, v["c4"])
    done_b3 = gather_z(8, rights[3].at[0, 0], 48, v["b3"])
    done_x1 = to_one(rights[1].at[0, 0], v["bx1"].at[pair], x_mate)
    v["bx1"][pair] = rights[1][0, 0]
    done_x0 = to_x(lambda other: rights[0].at[0, 0], v["bx0"])
    v["bx0"][x] = rights[0][0, 0]
    done_b = {}

    def more_b2():
        done_b[2] = gather_z(NZ, rights[2].at[0, 0], 24, v["b2"])

    def more_b1():
        done_x1()
        done_x0()
        done_b[1] = gather_z(NZ, v["bx1"], 24, v["b1"])
        done_b[0] = gather_z(NZ, v["bx0"], 24, v["b0"])

    done_b4()
    v["fp4"][...] = times(inverses[4][...], v["c4"][...])
    y4 = front_sum("f", 4, more_b2)
    v["u4"][...] = times(panels[4][...], y4[...])
    scatter_z(4, v["u4"], 32, v["ur4"])()
    v["us4"][...] = total(v["ur4"])
    done = gather_z(8, v["us4"], 32, v["ug4"])
    done_b3()
    done()

    place(3, v["b3"], v["ug4"][0:B, :], v["ug4"][B:, :])
    v["fp3"][...] = times(inverses[3][...], v["c3"][...])
    y3 = front_sum("f", 3, more_b1)
    v["u3"][...] = times(panels[3][...], y3[...]) + v["u4"][B:, :]
    scatter_z(8, v["u3"], 16, v["ur3"])()
    v["us3"][...] = total(v["ur3"])
    done = gather_z(NZ, v["us3"], 16, v["ug3"])
    done_b[2]()
    done()

    place(2, v["b2"], v["ug3"][0:B, :], v["ug3"][B:, :])
    v["fp2"][...] = times(inverses[2][...], v["c2"][...])
    y2 = front_sum("f", 2)
    v["u2"][...] = times(panels[2][...], y2[...]) + v["u3"][B:, :]
    scatter_z(NZ, v["u2"], 8, v["ur2"])()
    v["us2"][pair] = total(v["ur2"])
    to_one(v["us2"].at[pair], v["us2"].at[pair], x_mate)()
    done = gather_z(NZ, v["us2"], 16, v["ug2"])
    done_b[1]()
    for p in range(32):
        v["c1"][12 * p : 12 * p + 12, :] = v["b1"][p % 16, p // 16]
    done()

    low, high = (v["ug2"][:, j].reshape(B, 128) for j in range(2))
    place(1, v["c1"], low, high)
    v["fp1"][...] = times(inverses[1][...], v["c1"][...])
    y1 = front_sum("f", 1)
    v["u1"][...] = times(panels[1][...], y1[...]) + v["u2"][B:, :]
    scatter_z(NZ, v["u1"], 8, v["ur1"])()
    own = total(v["ur1"])
    v["uo1"][...] = own
    v["ux1"][x] = own
    to_x(lambda other: v["uo1"], v["ux1"])()
    v["us1"][0] = v["ux1"][0] + v["ux1"][1]
    v["us1"][1] = v["ux1"][2] + v["ux1"][3]
    done = gather_z(NZ, v["us1"], 16, v["ug1"])
    done_b[0]()
    for p in range(64):
        v["c0"][6 * p : 6 * p + 6, :] = v["b0"][p % 16, p // 16]
    done()

    low, high = (v["ug1"][:, j].reshape(B, 128) for j in range(2))
    place(0, v["c0"], low, high)
    v["fp0"][...] = times(inverses[0][...], v["c0"][...])
    y0 = front_sum("f", 0)

    def solve(level, right_side):
        v[f"s{level}"][...] = transposed_times(inverses[level][...], right_side)

    def picked(level):
        to_low, to_high = choices(level)
        s = v[f"s{level}"]
        return pick(s, to_low), pick(s, to_high)

    def remove(level, known, meanwhile=None):
        v[f"bp{level}"][...] = transposed_times(panels[level][...], known)
        through = front_sum("b", level, meanwhile)
        return v[f"fy{level}"][...] - through[...]

    answers = {}
    solve(0, y0[...])
    for j, rows in enumerate(picked(0)):
        v["k0"][:, j] = rows.reshape(16, 8, 128)
    scatter_z(NZ, v["k0"], 8, v["kr0"])()
    v["kx0"][...] = total(v["kr0"])
    done = to_x(lambda other: v["kx0"].at[other // 2], v["kt0"])
    v["kt0"][x] = v["kx0"][x // 2]
    done()
    v["ks0"][...] = total(v["kt0"])
    done = gather_z(NZ, v["ks0"], 8, v["z0"])
    done_a0 = to_x(lambda other: v["s0"].at[rows_of(other, 96)], v["ax0"])
    v["ax0"][x] = v["s0"][rows_of(x, 96), :]
    done()
    known = v["z0"][...].reshape(B, 128)

    def root_answer():
        done_a0()
        v["am0"][...] = total(v["ax0"])
        for p in range(16):
            v["ap0"][p] = v["am0"][6 * p : 6 * p + 6, :]
        answers[0] = scatter_z(NZ, v["ap0"], 6, v["ar0"])

    solve(1, remove(1, known, root_answer))
    for j, rows in enumerate(picked(1)):
        v["k1"][:, j] = rows.reshape(16, 8, 128)
    scatter_z(NZ, v["k1"], 8, v["kr1"])()
    v["kx1"][...] = total(v["kr1"])
    to_one(v["kx1"].at[1 - pair], v["kt1"], x_mate)()
    v["ks1"][...] = v["kx1"][pair] + v["kt1"][...]
    done = gather_z(NZ, v["ks1"], 8, v["z1"])
    done_a1 = to_one(v["s1"].at[rows_of(1 - pair, 192)], v["ax1"], x_mate)
    done()
    known = jnp.concatenate([v["z1"][...].reshape(B, 128), known], 0)

    def first_answer():
        done_a1()
        v["am1"][...] = v["s1"][rows_of(pair, 192), :] + v["ax1"][...]
        for p in range(16):
            v["ap1"][p] = v["am1"][12 * p : 12 * p + 12, :]
        answers[1] = scatter_z(NZ, v["ap1"], 12, v["ar1"])

    solve(2, remove(2, known, first_answer))
    for j, rows in enumerate(picked(2)):
        v["k2"][j * B : (j + 1) * B, :] = rows
    scatter_z(NZ, v["k2"], 16, v["kr2"])()
    v["ks2"][...] = total(v["kr2"])
    gather_z(8, v["ks2"], 16, v["z2"])()
    known = jnp.concatenate([v["z2"][...], known], 0)

    def second_answer():
        answers[2] = scatter_z(NZ, v["s2"], 24, v["ar2"])

    solve(3, remove(3, known, second_answer))
    for j, rows in enumerate(picked(3)):
        v["k3"][j * B : (j + 1) * B, :] = rows
    scatter_z(8, v["k3"], 32, v["kr3"])()
    v["ks3"][...] = total(v["kr3"])
    gather_z(4, v["ks3"], 32, v["z3"])()
    known = jnp.concatenate([v["z3"][...], known], 0)

    def third_answer():
        answers[3] = scatter_z(8, v["s3"], 48, v["ar3"])

    solve(4, remove(4, known, third_answer))
    answers[4] = scatter_z(4, v["s4"], 96, v["ar4"])
    for level in range(LEVELS):
        answers[level]()
        outs[level][0, 0] = total(v[f"ar{level}"])
    for like, k in sent:
        await_bytes(like, k, send_sems)


def per_device(added_rows, *arrays):
    vmem = pl.BlockSpec(memory_space=pltpu.VMEM)
    return pl.pallas_call(
        kernel,
        out_shape=tuple(jax.ShapeDtypeStruct((1, 1, w, 128), jnp.float32) for w in OWN),
        in_specs=[pl.BlockSpec(memory_space=pltpu.SMEM)] + [vmem] * 14,
        out_specs=(vmem,) * 5,
        scratch_shapes=[pltpu.VMEM(shape, jnp.float32) for shape in SCRATCH.values()]
        + [pltpu.SemaphoreType.DMA((SEMS,)), pltpu.SemaphoreType.DMA((SEMS,))],
        compiler_params=pltpu.CompilerParams(
            collective_id=0, has_side_effects=True, vmem_limit_bytes=48 * 2**20
        ),
        cost_estimate=pl.CostEstimate(flops=1_200_000_000, bytes_accessed=3_000_000, transcendentals=0),
        name="solve",
    )(added_rows, *arrays)


def solution(mesh):
    rights, inverses, panels = P("front", "leaf", None, None), P("leaf", "front"), P("front", "leaf")
    return jax.shard_map(
        per_device,
        mesh=mesh,
        in_specs=(P(),) + (rights,) * 5 + (inverses,) * 5 + (panels,) * 4,
        out_specs=(rights,) * 5,
        check_vma=False,
    )
```

time: 1340 us -> 260 us (0.19)
  waiting for transfers between devices: 920 us -> 0 us
  Pallas kernels: 0 us -> 246 us
  starting transfers between devices: 189 us -> 0 us
  blocking collectives: 168 us -> 0 us
  matrix products: 22.9 us -> 0 us
  between operations: 15.4 us -> 0.73 us
    psum x7 -> x0, waiting for transfers between devices: 697 us -> none  [the longest x1 246 us: group_total(): summed = lax.psum(slot_table, 'leaf')]
    pallas_call x0 -> x1, Pallas kernels: none -> 246 us  [per_device(): pl.pallas_call(kernel, out_shape=tuple((jax.ShapeDtypeStruct((1, 1, w, 12...]
    ppermute x46 -> x0, waiting for transfers between devices: 223 us -> none  [swapped(): return lax.ppermute(value, axis, pairs)]
    ppermute x46 -> x0, starting transfers between devices: 188 us -> none  [swapped(): return lax.ppermute(value, axis, pairs)]
    psum x3 -> x0, blocking collectives: 106 us -> none  [the longest x2 74.4 us: per_device(): solved = lax.psum(partial_rows, 'front')]
    all_gather x1 -> x0, blocking collectives: 61.7 us -> none  [group_gather(): whole_axis = lax.all_gather(own_piece, 'leaf', axis=0, tiled=True)]
    dot_general x22 -> x0, matrix products: 22.9 us -> none  [the longest x5 5.19 us: per_device(): jnp.dot(inverse_tile, slab, precision=exact_mode, preferred_element_type=...]
  transfers between devices with their start and end apart: 53 -> 0, of which waited for: 37 -> 0; matrix products, arithmetic and copies ran while one was open for 1% -> 0% of each run, Pallas kernels for 0% -> 0%
where the time goes in v1:
time: 260 us
  Pallas kernels  246 us (95%)
  local copies, waits for them, and re-layouts  12.7 us (5%)
    pallas_call x1, Pallas kernels, per_device(): pl.pallas_call(kernel, out_shape=tuple((jax.ShapeDtypeStruct((1, 1, w, 12...  246 us
    unnamed x28, local copies, waits for them, and re-layouts  11.5 us

profile of v1, /device:TPU:1, one launch (start us, length us, event | category | flops | bytes accessed | tf_op | source)
XLA Modules:
  0.0 259.7 jit_solution(8229639576654962124)
XLA Ops:
  0.6 0.0 copy-start.2
  0.6 0.7 copy.21.refs_0_
  1.4 0.7 copy.22.refs_1_
  2.1 0.8 copy.23.refs_10_
  2.9 0.8 copy.20.added
  3.8 0.0 copy-start.5
  3.8 0.0 copy-start.6
  3.8 0.0 copy-start.9
  3.8 1.0 copy.24.refs_11_
  4.8 0.0 copy-done.2
  4.8 0.0 copy-done.5
  4.8 0.0 copy-done.6
  4.9 0.0 copy-done.9
  4.9 0.0 copy-start
  4.9 1.1 copy-done
  6.0 0.0 copy-start.1
  6.0 1.1 copy-done.1
  7.1 0.0 copy-start.3
  7.1 1.0 copy-done.3
  8.0 0.0 copy-start.4
  8.0 0.9 copy-done.4
  8.9 0.0 copy-start.7
  8.9 0.8 copy-done.7
  9.7 0.0 copy-start.8
  9.7 0.7 copy-done.8
  10.4 246.2 %solve.1 = (f32[1,1,6,128]{3,2,1,0:T(8,128)S(1)}, f32[1,1,12,128]{3,2,1,0:T(8,128)S(1)}, f32[1,1,24,128]{3,2,1,0:T(8,128)S(1)}, f32[1,1,48,128]{3,2,1,0:T(8,128)S(1)}, f32[1,1,96,128]{3,2,1,0:T(8,128)S(1)}) custom-call(s32[30,8,1]{2,1,0:T(8,128)S(1)} %copy.20.added, f32[1,1,6,128]{3,2,1,0:T(8,128)S(1)} %copy.21.refs_0_, f32[1,1,12,128]{3,2,1,0:T(8,128)S(1)} %copy.22.refs_1_, ...), custom_call_target="tpu_custom_call" | custom-call | flops 1200000000 | bytes 3000000 | tf_op jit(solution)/shard_map/solve/pallas_call | solution.py:415
  256.7 0.6 copy.25
  257.3 0.6 copy.26
  257.9 0.6 copy.30
  258.5 0.6 copy.31
  259.1 0.6 copy.32
Async XLA Ops:
  0.6 4.2 %copy-start.2 = (bf16[384,384]{1,0:T(8,128)(2,1)S(1)}, bf16[384,384]{1,0:T(8,128)(2,1)}, u32[]{:S(2)}) copy-start(bf16[384,384]{1,0:T(8,128)(2,1)} %refs_8_.1) | copy-start | bytes 884740
  3.8 1.1 copy-start.5
  3.8 1.1 copy-start.6
  3.8 1.1 copy-start.9
  4.9 1.1 copy-start
  6.0 1.1 copy-start.1
  7.1 1.0 copy-start.3
  8.0 0.9 copy-start.4
  8.9 0.8 copy-start.7
  9.7 0.7 copy-start.8

commit v2 on v1

--- a/solution.py
+++ b/solution.py
@@ -39,7 +39,11 @@
         SCRATCH[f"{_way}p{_l}"] = (2 * _h, 128)
         SCRATCH[f"{_way}c{_l}"] = (_h, 128)
         SCRATCH[f"{_way}h{_l}"] = (_h, 128)
-        if _l >= 3:
+        if _l < 2:
+            SCRATCH[f"{_way}r{_l}"] = (4, 2 * _h, 128)
+            SCRATCH[f"{_way}h{_l}"] = (2 * _h, 128)
+            SCRATCH[f"{_way}g{_l}"] = (2 * _h, 128)
+        elif _l >= 3:
             SCRATCH[f"{_way}r{_l}"] = (4, _h // 4, 128)
             SCRATCH[f"{_way}q{_l}"] = (_h // 4, 128)
             SCRATCH[f"{_way}g{_l}"] = (_h, 128)
@@ -49,6 +53,13 @@
         SCRATCH[f"{_way}y{_l}"] = (2 * _h, 128)
 NAMES = tuple(SCRATCH)
 SEMS = 128
+MATRICES = {
+    "g0": (48, 384), "g1": (96, 384), "g2": (192, 384), "g3": (384, 384), "g4": (768, 384),
+    "q1": (96, 128), "q2": (192, 256), "p3": (384, 384), "p4": (512, 768),
+    "h0": (384, 48), "h1": (384, 96), "h2": (384, 192), "h3": (384, 384), "h4": (384, 768),
+    "p1": (128, 96), "p2": (256, 192), "q3": (384, 384), "q4": (768, 512),
+}
+LOADED = tuple(MATRICES)[:9]
 
 
 def split(values):
@@ -59,13 +70,6 @@
 
 def times(matrix, values):
     both = jnp.dot(matrix, split(values), preferred_element_type=jnp.float32)
-    return both[:, :128] + both[:, 128:]
-
-
-def transposed_times(matrix, values):
-    both = lax.dot_general(
-        matrix, split(values), (((0,), (0,)), ((), ())), preferred_element_type=jnp.float32
-    )
     return both[:, :128] + both[:, 128:]
 
 
@@ -81,12 +85,14 @@
 
 
 def kernel(added, *refs):
-    rights, refs = refs[:5], refs[5:]
-    inverses, refs = refs[:5], refs[5:]
-    panels, refs = (None,) + refs[:4], refs[4:]
+    stored_rights, refs = refs[:5], refs[5:]
+    stored, refs = refs[:9], refs[9:]
     outs, refs = refs[:5], refs[5:]
     v = dict(zip(NAMES, refs[: len(NAMES)]))
-    send_sems, recv_sems = refs[len(NAMES) :]
+    refs = refs[len(NAMES) :]
+    m = dict(zip(MATRICES, refs[: len(MATRICES)]))
+    rights, refs = refs[len(MATRICES) : len(MATRICES) + 5], refs[len(MATRICES) + 5 :]
+    send_sems, recv_sems, load_sems = refs
 
     leaf = lax.axis_index("leaf")
     front = lax.axis_index("front")
@@ -189,9 +195,21 @@
         return lambda: await_bytes(like, k, recv_sems)
 
     def front_sum(way, level, meanwhile=None):
-        term, from_core, half = v[f"{way}p{level}"], v[f"{way}c{level}"], v[f"{way}h{level}"]
-        received, summed, whole = v[f"{way}r{level}"], v[f"{way}g{level}"], v[f"{way}y{level}"]
+        term, half, whole = v[f"{way}p{level}"], v[f"{way}h{level}"], v[f"{way}y{level}"]
+        received, summed = v[f"{way}r{level}"], v[f"{way}g{level}"]
+        if level < 2:
+            done = to_y(lambda other: term, received.at[y], received.at[pl.ds(0, 3)])
+            received[y] = term[...]
+            if meanwhile is not None:
+                meanwhile()
+            done()
+            half[...] = total(received)
+            done = to_one(half, summed, core_mate)
+            done()
+            whole[...] = half[...] + summed[...]
+            return whole
         h = ROWS[level] // 2
+        from_core = v[f"{way}c{level}"]
         done = to_one(term.at[rows_of(1 - core, h)], from_core, core_mate)
         done()
         half[...] = term[rows_of(core, h), :] + from_core[...]
@@ -220,7 +238,7 @@
         return whole
 
     def choice(level, child):
-        block = added[2 ** (level + 1) - 2 + child, front, 0]
+        block = added[front, 0, 2 ** (level + 1) - 2 + child]
         return [jnp.where(block == j, 1.0, 0.0).astype(jnp.float32) for j in range(3)]
 
     def choices(level):
@@ -237,61 +255,102 @@
     def pick(s, weights):
         return s[0:B, :] * weights[0] + s[B : 2 * B, :] * weights[1] + s[2 * B :, :] * weights[2]
 
+    loads = {}
+
+    def load(name, src, dst, k):
+        copy = pltpu.make_async_copy(src, dst, load_sems.at[k])
+        copy.start()
+        loads[name] = copy.wait
+
+    load("r4", stored_rights[4].at[0, 0], rights[4], 4)
+    load("g4", stored[4], m["g4"], 9)
+    for level in (3, 2):
+        load(f"r{level}", stored_rights[level].at[0, 0], rights[level], level)
+    for level in (1, 0):
+        for i in range(OWN[level]):
+            pltpu.make_async_copy(
+                stored_rights[level].at[0, i], rights[level].at[pl.ds(i, 1)], load_sems.at[level]
+            ).start()
+    for k, name in enumerate(LOADED):
+        if name != "g4":
+            load(name, stored[k], m[name], 5 + k)
+
     barrier = pltpu.get_barrier_semaphore()
 
-    def greet(i, _):
-        _, device = at_z(NZ, i)
+    def greet(device):
         pl.semaphore_signal(barrier, inc=1, device_id=device, device_id_type=MESH)
-        return 0
-
-    lax.fori_loop(0, NZ - 1, greet, 0)
+
+    greet((x * NZ + (z + 4) % NZ, front))
+    greet((x * NZ + (z + 12) % NZ, front))
+    for i in range(3):
+        greet(at_z(4, i)[1])
     for d in (1, 2, 3):
-        pl.semaphore_signal(barrier, inc=1, device_id=at_x(d)[1], device_id_type=MESH)
-        pl.semaphore_signal(barrier, inc=1, device_id=at_y(d)[1], device_id_type=MESH)
-    pl.semaphore_signal(barrier, inc=1, device_id=core_mate, device_id_type=MESH)
-    pl.semaphore_wait(barrier, NZ - 1 + 7)
-
-    done_b4 = gather_z(4, rights[4].at[0, 0], 96, v["c4"])
-    done_b3 = gather_z(8, rights[3].at[0, 0], 48, v["b3"])
-    done_x1 = to_one(rights[1].at[0, 0], v["bx1"].at[pair], x_mate)
-    v["bx1"][pair] = rights[1][0, 0]
-    done_x0 = to_x(lambda other: rights[0].at[0, 0], v["bx0"])
-    v["bx0"][x] = rights[0][0, 0]
+        greet(at_x(d)[1])
+        greet(at_y(d)[1])
+    greet(core_mate)
+    pl.semaphore_wait(barrier, 12)
+
+    loads["r4"]()
+    done_b4 = gather_z(4, rights[4], 96, v["c4"])
+    await_bytes(rights[1], 1, load_sems)
+    done_x1 = to_one(rights[1], v["bx1"].at[pair], x_mate)
+    v["bx1"][pair] = rights[1][...]
+    await_bytes(rights[0], 0, load_sems)
+    done_x0 = to_x(lambda other: rights[0], v["bx0"])
+    v["bx0"][x] = rights[0][...]
+    for name in ("r3", "r2") + LOADED:
+        loads[name]()
     done_b = {}
 
+    def turn(*names):
+        for source, target in names:
+            m[target][...] = m[source][...].T
+
+    def more_b3():
+        done_b[3] = gather_z(8, rights[3], 48, v["b3"])
+
     def more_b2():
-        done_b[2] = gather_z(NZ, rights[2].at[0, 0], 24, v["b2"])
+        done_b[2] = gather_z(NZ, rights[2], 24, v["b2"])
 
     def more_b1():
         done_x1()
+        done_b[1] = gather_z(NZ, v["bx1"], 24, v["b1"])
+
+    def more_b0():
         done_x0()
-        done_b[1] = gather_z(NZ, v["bx1"], 24, v["b1"])
         done_b[0] = gather_z(NZ, v["bx0"], 24, v["b0"])
 
+    turn(("g4", "h4"))
     done_b4()
-    v["fp4"][...] = times(inverses[4][...], v["c4"][...])
-    y4 = front_sum("f", 4, more_b2)
-    v["u4"][...] = times(panels[4][...], y4[...])
-    scatter_z(4, v["u4"], 32, v["ur4"])()
+    v["fp4"][...] = times(m["g4"][...], v["c4"][...])
+    y4 = front_sum("f", 4, more_b3)
+    v["u4"][...] = times(m["p4"][...], y4[...])
+    done = scatter_z(4, v["u4"], 32, v["ur4"])
+    turn(("p4", "q4"))
+    done()
     v["us4"][...] = total(v["ur4"])
     done = gather_z(8, v["us4"], 32, v["ug4"])
-    done_b3()
+    turn(("g3", "h3"), ("q2", "p2"), ("q1", "p1"))
+    done_b[3]()
     done()
 
     place(3, v["b3"], v["ug4"][0:B, :], v["ug4"][B:, :])
-    v["fp3"][...] = times(inverses[3][...], v["c3"][...])
-    y3 = front_sum("f", 3, more_b1)
-    v["u3"][...] = times(panels[3][...], y3[...]) + v["u4"][B:, :]
-    scatter_z(8, v["u3"], 16, v["ur3"])()
+    v["fp3"][...] = times(m["g3"][...], v["c3"][...])
+    y3 = front_sum("f", 3, more_b2)
+    v["u3"][...] = times(m["p3"][...], y3[...]) + v["u4"][B:, :]
+    done = scatter_z(8, v["u3"], 16, v["ur3"])
+    turn(("p3", "q3"))
+    done()
     v["us3"][...] = total(v["ur3"])
     done = gather_z(NZ, v["us3"], 16, v["ug3"])
+    turn(("g2", "h2"), ("g1", "h1"), ("g0", "h0"))
     done_b[2]()
     done()
 
     place(2, v["b2"], v["ug3"][0:B, :], v["ug3"][B:, :])
-    v["fp2"][...] = times(inverses[2][...], v["c2"][...])
-    y2 = front_sum("f", 2)
-    v["u2"][...] = times(panels[2][...], y2[...]) + v["u3"][B:, :]
+    v["fp2"][...] = times(m["g2"][...], v["c2"][...])
+    y2 = front_sum("f", 2, more_b1)
+    v["u2"][...] = times(m["p2"][...], y2[...]) + v["u3"][B:, :]
     scatter_z(NZ, v["u2"], 8, v["ur2"])()
     v["us2"][pair] = total(v["ur2"])
     to_one(v["us2"].at[pair], v["us2"].at[pair], x_mate)()
@@ -303,9 +362,9 @@
 
     low, high = (v["ug2"][:, j].reshape(B, 128) for j in range(2))
     place(1, v["c1"], low, high)
-    v["fp1"][...] = times(inverses[1][...], v["c1"][...])
-    y1 = front_sum("f", 1)
-    v["u1"][...] = times(panels[1][...], y1[...]) + v["u2"][B:, :]
+    v["fp1"][...] = times(m["g1"][...], v["c1"][...])
+    y1 = front_sum("f", 1, more_b0)
+    v["u1"][...] = times(m["p1"][...], y1[...]) + v["u2"][B:, :]
     scatter_z(NZ, v["u1"], 8, v["ur1"])()
     own = total(v["ur1"])
     v["uo1"][...] = own
@@ -321,11 +380,11 @@
 
     low, high = (v["ug1"][:, j].reshape(B, 128) for j in range(2))
     place(0, v["c0"], low, high)
-    v["fp0"][...] = times(inverses[0][...], v["c0"][...])
+    v["fp0"][...] = times(m["g0"][...], v["c0"][...])
     y0 = front_sum("f", 0)
 
     def solve(level, right_side):
-        v[f"s{level}"][...] = transposed_times(inverses[level][...], right_side)
+        v[f"s{level}"][...] = times(m[f"h{level}"][...], right_side)
 
     def picked(level):
         to_low, to_high = choices(level)
@@ -333,7 +392,7 @@
         return pick(s, to_low), pick(s, to_high)
 
     def remove(level, known, meanwhile=None):
-        v[f"bp{level}"][...] = transposed_times(panels[level][...], known)
+        v[f"bp{level}"][...] = times(m[f"q{level}"][...], known)
         through = front_sum("b", level, meanwhile)
         return v[f"fy{level}"][...] - through[...]
 
@@ -410,21 +469,23 @@
         await_bytes(like, k, send_sems)
 
 
-def per_device(added_rows, *arrays):
+def per_device(added_rows, r0, r1, r2, r3, r4, g0, g1, g2, g3, g4, p1, p2, p3, p4):
     vmem = pl.BlockSpec(memory_space=pltpu.VMEM)
     return pl.pallas_call(
         kernel,
         out_shape=tuple(jax.ShapeDtypeStruct((1, 1, w, 128), jnp.float32) for w in OWN),
-        in_specs=[pl.BlockSpec(memory_space=pltpu.SMEM)] + [vmem] * 14,
+        in_specs=[pl.BlockSpec(memory_space=pltpu.SMEM)] + [pl.BlockSpec(memory_space=pl.ANY)] * 14,
         out_specs=(vmem,) * 5,
         scratch_shapes=[pltpu.VMEM(shape, jnp.float32) for shape in SCRATCH.values()]
-        + [pltpu.SemaphoreType.DMA((SEMS,)), pltpu.SemaphoreType.DMA((SEMS,))],
+        + [pltpu.VMEM(shape, jnp.bfloat16) for shape in MATRICES.values()]
+        + [pltpu.VMEM((w, 128), jnp.float32) for w in OWN]
+        + [pltpu.SemaphoreType.DMA((SEMS,)), pltpu.SemaphoreType.DMA((SEMS,)), pltpu.SemaphoreType.DMA((14,))],
         compiler_params=pltpu.CompilerParams(
-            collective_id=0, has_side_effects=True, vmem_limit_bytes=48 * 2**20
+            collective_id=0, has_side_effects=True, vmem_limit_bytes=57 * 2**20
         ),
         cost_estimate=pl.CostEstimate(flops=1_200_000_000, bytes_accessed=3_000_000, transcendentals=0),
         name="solve",
-    )(added_rows, *arrays)
+    )(added_rows.transpose(1, 2, 0), r0.transpose(0, 2, 1, 3), r1.transpose(0, 2, 1, 3), r2, r3, r4, g0, g1, g2, g3, g4, p1.T, p2.T, p3, p4)
 
 
 def solution(mesh):

time: 260 us -> 240 us (0.923)
  Pallas kernels: 246 us -> 236 us
  local copies, waits for them, and re-layouts: 12.7 us -> 3.73 us
    pallas_call x1, Pallas kernels: 246 us -> 236 us  [per_device(): pl.pallas_call(kernel, out_shape=tuple((jax.ShapeDtypeStruct((1, 1, w, 12...]
    unnamed x28 -> x11, local copies, waits for them, and re-layouts: 11.5 us -> 1.84 us
where the time goes in v2:
time: 240 us
  Pallas kernels  236 us (98%)
  local copies, waits for them, and re-layouts  3.73 us (2%)
    pallas_call x1, Pallas kernels, per_device(): pl.pallas_call(kernel, out_shape=tuple((jax.ShapeDtypeStruct((1, 1, w, 12...  236 us

profile of v2, /device:TPU:1, one launch (start us, length us, event | category | flops | bytes accessed | tf_op | source)
XLA Modules:
  0.0 240.1 jit_solution(13184498511858901322)
XLA Ops:
  0.6 235.7 %solve.1 = (f32[1,1,6,128]{3,2,1,0:T(8,128)}, f32[1,1,12,128]{3,2,1,0:T(8,128)}, f32[1,1,24,128]{3,2,1,0:T(8,128)}, f32[1,1,48,128]{3,2,1,0:T(8,128)}, f32[1,1,96,128]{3,2,1,0:T(8,128)}) custom-call(s32[8,1,30]{2,1,0:T(1,128)} %bitcast.8, f32[1,6,1,128]{3,2,1,0:T(1,128)} %bitcast.9, f32[1,12,1,128]{3,2,1,0:T(1,128)} %bitcast.7, f32[1,1,24,128]{3,2,1,0:T(8,128)} %refs_2_.1, ...), custom_call_target="tpu_custom_call" | custom-call | flops 1200000000 | bytes 3000000 | tf_op jit(solution)/shard_map/solve/pallas_call | solution.py:474
  236.3 0.0 copy-start.3
  236.3 0.0 copy-start.2
  236.3 0.0 copy-start.1
  236.4 0.0 copy-start
  236.4 1.3 copy.20
  237.7 0.0 copy-done.3
  237.7 0.6 copy.21
  238.3 0.0 copy-done.2
  238.3 0.6 copy.25
  238.9 0.0 copy-done.1
  238.9 0.6 copy.26
  239.5 0.0 copy-done
  239.5 0.6 copy.27
Async XLA Ops:
  236.3 1.3 copy-start.3
  236.3 1.9 copy-start.2
  236.3 2.5 %copy-start.1 = (f32[1,1,48,128]{3,2,1,0:T(8,128)S(1)}, f32[1,1,48,128]{3,2,1,0:T(8,128)}, u32[]{:S(2)}) copy-start(f32[1,1,48,128]{3,2,1,0:T(8,128)} %get-tuple-element.18) | copy-start | bytes 73732
  236.4 3.1 %copy-start = (f32[1,1,96,128]{3,2,1,0:T(8,128)S(1)}, f32[1,1,96,128]{3,2,1,0:T(8,128)}, u32[]{:S(2)}) copy-start(f32[1,1,96,128]{3,2,1,0:T(8,128)} %get-tuple-element.19) | copy-start | bytes 147460

commit v3 on v2

--- a/solution.py
+++ b/solution.py
@@ -12,26 +12,26 @@
 NX = 4
 NY = 4
 SLAB = 384
-ROWS = (48, 96, 192, 384, 768)
+ROWS = (192, 192, 192, 384, 768)
 OWN = (6, 12, 24, 48, 96)
 
 SCRATCH = {
-    "bx0": (4, 6, 128), "bx1": (2, 12, 128),
-    "b0": (16, 4, 6, 128), "b1": (16, 2, 12, 128), "b2": (SLAB, 128), "b3": (SLAB, 128), "c4": (SLAB, 128),
+    "b0": (4, 16, 6, 128), "b1": (2, 16, 12, 128), "b2": (SLAB, 128), "b3": (SLAB, 128), "c4": (SLAB, 128),
     "c3": (SLAB, 128), "c2": (SLAB, 128), "c1": (SLAB, 128), "c0": (SLAB, 128),
-    "u4": (512, 128), "u3": (384, 128), "u2": (256, 128), "u1": (128, 128),
+    "t0": (4, 48, 384), "t1": (2, 96, 384), "tp": (2, 96, 128),
+    "u4": (512, 128), "u3": (384, 128), "u2": (256, 128), "u2x": (128, 128), "u1": (128, 128),
     "ur4": (4, 32, 128), "us4": (32, 128), "ug4": (256, 128),
     "ur3": (8, 16, 128), "us3": (16, 128), "ug3": (256, 128),
-    "ur2": (16, 8, 128), "us2": (2, 8, 128), "ug2": (16, 2, 8, 128),
-    "ur1": (16, 8, 128), "ux1": (4, 8, 128), "uo1": (8, 128), "us1": (2, 8, 128), "ug1": (16, 2, 8, 128),
+    "ur2": (16, 8, 128), "us2": (8, 128), "ug2": (2, 16, 8, 128),
+    "ur1": (16, 8, 128), "us1": (8, 128), "ug1": (2, 16, 8, 128),
     "s0": (SLAB, 128), "s1": (SLAB, 128), "s2": (SLAB, 128), "s3": (SLAB, 128), "s4": (SLAB, 128),
-    "k0": (16, 2, 8, 128), "kr0": (16, 2, 8, 128), "kx0": (2, 8, 128), "kt0": (4, 8, 128), "ks0": (8, 128), "z0": (16, 8, 128),
-    "k1": (16, 2, 8, 128), "kr1": (16, 2, 8, 128), "kx1": (2, 8, 128), "kt1": (8, 128), "ks1": (8, 128), "z1": (16, 8, 128),
+    "k0": (128, 128), "kr0": (16, 8, 128), "ks0": (8, 128), "z0": (128, 128),
+    "k1": (128, 128), "kr1": (16, 8, 128), "ks1": (8, 128), "z1": (128, 128),
     "k2": (256, 128), "kr2": (16, 16, 128), "ks2": (16, 128), "z2": (128, 128),
     "k3": (256, 128), "kr3": (8, 32, 128), "ks3": (32, 128), "z3": (128, 128),
     "ar4": (4, 96, 128), "ar3": (8, 48, 128), "ar2": (16, 24, 128),
-    "ax1": (192, 128), "am1": (192, 128), "ap1": (16, 12, 128), "ar1": (16, 12, 128),
-    "ax0": (4, 96, 128), "am0": (96, 128), "ap0": (16, 6, 128), "ar0": (16, 6, 128),
+    "am1": (192, 128), "ap1": (16, 12, 128), "ar1": (16, 12, 128),
+    "am0": (96, 128), "ap0": (16, 6, 128), "ar0": (16, 6, 128),
 }
 for _way in "fb":
     for _l in range(LEVELS):
@@ -39,11 +39,7 @@
         SCRATCH[f"{_way}p{_l}"] = (2 * _h, 128)
         SCRATCH[f"{_way}c{_l}"] = (_h, 128)
         SCRATCH[f"{_way}h{_l}"] = (_h, 128)
-        if _l < 2:
-            SCRATCH[f"{_way}r{_l}"] = (4, 2 * _h, 128)
-            SCRATCH[f"{_way}h{_l}"] = (2 * _h, 128)
-            SCRATCH[f"{_way}g{_l}"] = (2 * _h, 128)
-        elif _l >= 3:
+        if _l >= 3:
             SCRATCH[f"{_way}r{_l}"] = (4, _h // 4, 128)
             SCRATCH[f"{_way}q{_l}"] = (_h // 4, 128)
             SCRATCH[f"{_way}g{_l}"] = (_h, 128)
@@ -54,10 +50,11 @@
 NAMES = tuple(SCRATCH)
 SEMS = 128
 MATRICES = {
-    "g0": (48, 384), "g1": (96, 384), "g2": (192, 384), "g3": (384, 384), "g4": (768, 384),
-    "q1": (96, 128), "q2": (192, 256), "p3": (384, 384), "p4": (512, 768),
-    "h0": (384, 48), "h1": (384, 96), "h2": (384, 192), "h3": (384, 384), "h4": (384, 768),
-    "p1": (128, 96), "p2": (256, 192), "q3": (384, 384), "q4": (768, 512),
+    "g0x": (48, 384), "g1x": (96, 384), "g2": (192, 384), "g3": (384, 384), "g4": (768, 384),
+    "q1x": (96, 128), "q2": (192, 256), "p3": (384, 384), "p4": (512, 768),
+    "g0": (192, 384), "g1": (192, 384), "q1": (192, 128),
+    "h0": (384, 192), "h1": (384, 192), "h2": (384, 192), "h3": (384, 384), "h4": (384, 768),
+    "p1": (128, 192), "p2": (256, 192), "q3": (384, 384), "q4": (768, 512),
 }
 LOADED = tuple(MATRICES)[:9]
 
@@ -171,6 +168,27 @@
         sent.append((like, k))
         return lambda: await_bytes(like, k, recv_sems)
 
+    def gather_xz(src, dst, slot, other_x):
+        k, k_other = begin(), begin()
+
+        def step(i, _):
+            there, device = at_z(NZ, i)
+            send(src, dst.at[slot, z], k_other, (other_x * NZ + there, front))
+            send(src, dst.at[slot, z], k, device)
+            return 0
+
+        lax.fori_loop(0, NZ - 1, step, 0)
+        send(src, dst.at[slot, z], k_other, (other_x * NZ + z, front))
+        dst[slot, z] = src[...]
+        sent.append((dst.at[0, pl.ds(0, NZ - 1)], k))
+        sent.append((dst.at[0], k_other))
+
+        def done():
+            await_bytes(dst.at[0, pl.ds(0, NZ - 1)], k, recv_sems)
+            await_bytes(dst.at[0], k_other, recv_sems)
+
+        return done
+
     def to_one(src, dst, device):
         k = begin()
         send(src, dst, k, device)
@@ -197,17 +215,6 @@
     def front_sum(way, level, meanwhile=None):
         term, half, whole = v[f"{way}p{level}"], v[f"{way}h{level}"], v[f"{way}y{level}"]
         received, summed = v[f"{way}r{level}"], v[f"{way}g{level}"]
-        if level < 2:
-            done = to_y(lambda other: term, received.at[y], received.at[pl.ds(0, 3)])
-            received[y] = term[...]
-            if meanwhile is not None:
-                meanwhile()
-            done()
-            half[...] = total(received)
-            done = to_one(half, summed, core_mate)
-            done()
-            whole[...] = half[...] + summed[...]
-            return whole
         h = ROWS[level] // 2
         from_core = v[f"{way}c{level}"]
         done = to_one(term.at[rows_of(1 - core, h)], from_core, core_mate)
@@ -293,13 +300,17 @@
     loads["r4"]()
     done_b4 = gather_z(4, rights[4], 96, v["c4"])
     await_bytes(rights[1], 1, load_sems)
-    done_x1 = to_one(rights[1], v["bx1"].at[pair], x_mate)
-    v["bx1"][pair] = rights[1][...]
     await_bytes(rights[0], 0, load_sems)
-    done_x0 = to_x(lambda other: rights[0], v["bx0"])
-    v["bx0"][x] = rights[0][...]
     for name in ("r3", "r2") + LOADED:
         loads[name]()
+    v["t0"][x] = m["g0x"][...].astype(jnp.float32)
+    v["t1"][pair] = m["g1x"][...].astype(jnp.float32)
+    v["tp"][pair] = m["q1x"][...].astype(jnp.float32)
+    done_tiles = [
+        to_x(lambda other: v["t0"].at[x], v["t0"]),
+        to_one(v["t1"].at[pair], v["t1"].at[pair], x_mate),
+        to_one(v["tp"].at[pair], v["tp"].at[pair], x_mate),
+    ]
     done_b = {}
 
     def turn(*names):
@@ -313,12 +324,10 @@
         done_b[2] = gather_z(NZ, rights[2], 24, v["b2"])
 
     def more_b1():
-        done_x1()
-        done_b[1] = gather_z(NZ, v["bx1"], 24, v["b1"])
+        done_b[1] = gather_z(NZ, rights[1], 12, v["b1"].at[pair])
 
     def more_b0():
-        done_x0()
-        done_b[0] = gather_z(NZ, v["bx0"], 24, v["b0"])
+        done_b[0] = gather_z(NZ, rights[0], 6, v["b0"].at[x])
 
     turn(("g4", "h4"))
     done_b4()
@@ -330,7 +339,7 @@
     done()
     v["us4"][...] = total(v["ur4"])
     done = gather_z(8, v["us4"], 32, v["ug4"])
-    turn(("g3", "h3"), ("q2", "p2"), ("q1", "p1"))
+    turn(("g3", "h3"), ("q2", "p2"))
     done_b[3]()
     done()
 
@@ -343,7 +352,12 @@
     done()
     v["us3"][...] = total(v["ur3"])
     done = gather_z(NZ, v["us3"], 16, v["ug3"])
-    turn(("g2", "h2"), ("g1", "h1"), ("g0", "h0"))
+    for wait in done_tiles:
+        wait()
+    m["g0"][...] = v["t0"][...].reshape(192, 384).astype(jnp.bfloat16)
+    m["g1"][...] = v["t1"][...].reshape(192, 384).astype(jnp.bfloat16)
+    m["q1"][...] = v["tp"][...].reshape(192, 128).astype(jnp.bfloat16)
+    turn(("g2", "h2"), ("g1", "h1"), ("g0", "h0"), ("q1", "p1"))
     done_b[2]()
     done()
 
@@ -352,33 +366,31 @@
     y2 = front_sum("f", 2, more_b1)
     v["u2"][...] = times(m["p2"][...], y2[...]) + v["u3"][B:, :]
     scatter_z(NZ, v["u2"], 8, v["ur2"])()
-    v["us2"][pair] = total(v["ur2"])
-    to_one(v["us2"].at[pair], v["us2"].at[pair], x_mate)()
-    done = gather_z(NZ, v["us2"], 16, v["ug2"])
+    v["us2"][...] = total(v["ur2"])
+    done = gather_xz(v["us2"], v["ug2"], pair, x + 1 - 2 * pair)
+    done_u2x = to_one(v["u2"].at[pl.ds(B, B)], v["u2x"], x_mate)
     done_b[1]()
+    to_one(v["b1"].at[pair], v["b1"].at[pair], x_mate)()
     for p in range(32):
-        v["c1"][12 * p : 12 * p + 12, :] = v["b1"][p % 16, p // 16]
-    done()
-
-    low, high = (v["ug2"][:, j].reshape(B, 128) for j in range(2))
+        v["c1"][12 * p : 12 * p + 12, :] = v["b1"][p // 16, p % 16]
+    done()
+
+    low, high = (v["ug2"][j].reshape(B, 128) for j in range(2))
     place(1, v["c1"], low, high)
     v["fp1"][...] = times(m["g1"][...], v["c1"][...])
     y1 = front_sum("f", 1, more_b0)
-    v["u1"][...] = times(m["p1"][...], y1[...]) + v["u2"][B:, :]
+    done_u2x()
+    v["u1"][...] = times(m["p1"][...], y1[...]) + (v["u2"][B:, :] + v["u2x"][...])
     scatter_z(NZ, v["u1"], 8, v["ur1"])()
-    own = total(v["ur1"])
-    v["uo1"][...] = own
-    v["ux1"][x] = own
-    to_x(lambda other: v["uo1"], v["ux1"])()
-    v["us1"][0] = v["ux1"][0] + v["ux1"][1]
-    v["us1"][1] = v["ux1"][2] + v["ux1"][3]
-    done = gather_z(NZ, v["us1"], 16, v["ug1"])
+    v["us1"][...] = total(v["ur1"])
+    done = gather_xz(v["us1"], v["ug1"], x // 2, (x + 2) % NX)
     done_b[0]()
+    to_x(lambda other: v["b0"].at[x], v["b0"])()
     for p in range(64):
-        v["c0"][6 * p : 6 * p + 6, :] = v["b0"][p % 16, p // 16]
-    done()
-
-    low, high = (v["ug1"][:, j].reshape(B, 128) for j in range(2))
+        v["c0"][6 * p : 6 * p + 6, :] = v["b0"][p // 16, p % 16]
+    done()
+
+    low, high = (v["ug1"][j].reshape(B, 128) for j in range(2))
     place(0, v["c0"], low, high)
     v["fp0"][...] = times(m["g0"][...], v["c0"][...])
     y0 = front_sum("f", 0)
@@ -398,42 +410,27 @@
 
     answers = {}
     solve(0, y0[...])
-    for j, rows in enumerate(picked(0)):
-        v["k0"][:, j] = rows.reshape(16, 8, 128)
+    v["k0"][...] = pick(v["s0"], choice(0, x // 2))
     scatter_z(NZ, v["k0"], 8, v["kr0"])()
-    v["kx0"][...] = total(v["kr0"])
-    done = to_x(lambda other: v["kx0"].at[other // 2], v["kt0"])
-    v["kt0"][x] = v["kx0"][x // 2]
-    done()
-    v["ks0"][...] = total(v["kt0"])
-    done = gather_z(NZ, v["ks0"], 8, v["z0"])
-    done_a0 = to_x(lambda other: v["s0"].at[rows_of(other, 96)], v["ax0"])
-    v["ax0"][x] = v["s0"][rows_of(x, 96), :]
-    done()
-    known = v["z0"][...].reshape(B, 128)
+    v["ks0"][...] = total(v["kr0"])
+    gather_z(NZ, v["ks0"], 8, v["z0"])()
+    known = v["z0"][...]
 
     def root_answer():
-        done_a0()
-        v["am0"][...] = total(v["ax0"])
+        v["am0"][...] = v["s0"][rows_of(x, 96), :]
         for p in range(16):
             v["ap0"][p] = v["am0"][6 * p : 6 * p + 6, :]
         answers[0] = scatter_z(NZ, v["ap0"], 6, v["ar0"])
 
     solve(1, remove(1, known, root_answer))
-    for j, rows in enumerate(picked(1)):
-        v["k1"][:, j] = rows.reshape(16, 8, 128)
+    v["k1"][...] = pick(v["s1"], choice(1, x))
     scatter_z(NZ, v["k1"], 8, v["kr1"])()
-    v["kx1"][...] = total(v["kr1"])
-    to_one(v["kx1"].at[1 - pair], v["kt1"], x_mate)()
-    v["ks1"][...] = v["kx1"][pair] + v["kt1"][...]
-    done = gather_z(NZ, v["ks1"], 8, v["z1"])
-    done_a1 = to_one(v["s1"].at[rows_of(1 - pair, 192)], v["ax1"], x_mate)
-    done()
-    known = jnp.concatenate([v["z1"][...].reshape(B, 128), known], 0)
+    v["ks1"][...] = total(v["kr1"])
+    gather_z(NZ, v["ks1"], 8, v["z1"])()
+    known = jnp.concatenate([v["z1"][...], known], 0)
 
     def first_answer():
-        done_a1()
-        v["am1"][...] = v["s1"][rows_of(pair, 192), :] + v["ax1"][...]
+        v["am1"][...] = v["s1"][rows_of(pair, 192), :]
         for p in range(16):
             v["ap1"][p] = v["am1"][12 * p : 12 * p + 12, :]
         answers[1] = scatter_z(NZ, v["ap1"], 12, v["ar1"])

time: 240 us -> 227 us (0.946)
  Pallas kernels: 236 us -> 222 us
    pallas_call x1, Pallas kernels: 236 us -> 222 us  [per_device(): pl.pallas_call(kernel, out_shape=tuple((jax.ShapeDtypeStruct((1, 1, w, 12...]
where the time goes in v3:
time: 227 us
  Pallas kernels  222 us (98%)
  local copies, waits for them, and re-layouts  3.73 us (2%)
    pallas_call x1, Pallas kernels, per_device(): pl.pallas_call(kernel, out_shape=tuple((jax.ShapeDtypeStruct((1, 1, w, 12...  222 us

profile of v3, /device:TPU:1, one launch (start us, length us, event | category | flops | bytes accessed | tf_op | source)
XLA Modules:
  0.0 226.8 jit_solution(11454685796266258170)
XLA Ops:
  0.6 222.4 %solve.1 = (f32[1,1,6,128]{3,2,1,0:T(8,128)}, f32[1,1,12,128]{3,2,1,0:T(8,128)}, f32[1,1,24,128]{3,2,1,0:T(8,128)}, f32[1,1,48,128]{3,2,1,0:T(8,128)}, f32[1,1,96,128]{3,2,1,0:T(8,128)}) custom-call(s32[8,1,30]{2,1,0:T(1,128)} %bitcast.8, f32[1,6,1,128]{3,2,1,0:T(1,128)} %bitcast.9, f32[1,12,1,128]{3,2,1,0:T(1,128)} %bitcast.7, f32[1,1,24,128]{3,2,1,0:T(8,128)} %refs_2_.1, ...), custom_call_target="tpu_custom_call" | custom-call | flops 1200000000 | bytes 3000000 | tf_op jit(solution)/shard_map/solve/pallas_call | solution.py:471
  223.1 0.0 copy-start.3
  223.1 0.0 copy-start.2
  223.1 0.0 copy-start.1
  223.1 0.0 copy-start
  223.1 1.3 copy.20
  224.4 0.0 copy-done.3
  224.4 0.6 copy.21
  225.0 0.0 copy-done.2
  225.0 0.6 copy.25
  225.6 0.0 copy-done.1
  225.6 0.6 copy.26
  226.2 0.0 copy-done
  226.2 0.6 copy.27
Async XLA Ops:
  223.1 1.3 copy-start.3
  223.1 1.9 copy-start.2
  223.1 2.5 %copy-start.1 = (f32[1,1,48,128]{3,2,1,0:T(8,128)S(1)}, f32[1,1,48,128]{3,2,1,0:T(8,128)}, u32[]{:S(2)}) copy-start(f32[1,1,48,128]{3,2,1,0:T(8,128)} %get-tuple-element.18) | copy-start | bytes 73732
  223.1 3.1 %copy-start = (f32[1,1,96,128]{3,2,1,0:T(8,128)S(1)}, f32[1,1,96,128]{3,2,1,0:T(8,128)}, u32[]{:S(2)}) copy-start(f32[1,1,96,128]{3,2,1,0:T(8,128)} %get-tuple-element.19) | copy-start | bytes 147460

commit v4 on v3

--- a/solution.py
+++ b/solution.py
@@ -93,27 +93,38 @@
 
     leaf = lax.axis_index("leaf")
     front = lax.axis_index("front")
-    x, z = leaf // NZ, leaf % NZ
-    y, core = front // 2, front % 2
-    pair = x % 2
+    x, z = lax.div(leaf, NZ), lax.rem(leaf, NZ)
+    y, core = lax.div(front, 2), lax.rem(front, 2)
+    pair = lax.rem(x, 2)
 
     counter = [0]
     sent = []
 
-    def at_z(n, i):
-        d = n // 2 + (i + 1) // 2 * (1 - 2 * (i % 2))
-        there = (z % n + d) % n
-        return there, (x * NZ + z - z % n + there, front)
+    def each_z(n, act):
+        here = lax.rem(z, n)
+        start = leaf - here
+
+        def partner(d):
+            there = lax.rem(here + d, n)
+            act(there, start + there)
+
+        def step(k, _):
+            partner(n // 2 - k)
+            partner(n // 2 + k)
+            return 0
+
+        partner(n // 2)
+        lax.fori_loop(1, n // 2, step, 0)
 
     def at_x(d):
-        other = (x + d) % NX
+        other = lax.rem(x + d, NX)
         return other, (other * NZ + z, front)
 
     x_mate = ((x + 1 - 2 * pair) * NZ + z, front)
     core_mate = (leaf, front + 1 - 2 * core)
 
     def at_y(d):
-        other = (y + d) % NY
+        other = lax.rem(y + d, NY)
         return other, (leaf, other * 2 + core)
 
     def begin():
@@ -136,13 +147,8 @@
         def piece(i):
             return src.at[i] if whole_pieces else src.at[rows_of(i, rows)]
 
-        def step(i, _):
-            there, device = at_z(n, i)
-            send(piece(there), dst.at[z % n], k, device)
-            return 0
-
-        lax.fori_loop(0, n - 1, step, 0)
-        here = z % n
+        here = lax.rem(z, n)
+        each_z(n, lambda there, device: send(piece(there), dst.at[here], k, (device, front)))
         dst[here] = src[here] if whole_pieces else src[rows_of(here, rows), :]
         like = dst.at[pl.ds(0, n - 1)]
         sent.append((like, k))
@@ -151,15 +157,10 @@
     def gather_z(n, src, rows, dst):
         k = begin()
         whole_pieces = len(dst.shape) > 2
-        here = z % n
+        here = lax.rem(z, n)
         spot = dst.at[here] if whole_pieces else dst.at[rows_of(here, rows)]
 
-        def step(i, _):
-            _, device = at_z(n, i)
-            send(src, spot, k, device)
-            return 0
-
-        lax.fori_loop(0, n - 1, step, 0)
+        each_z(n, lambda there, device: send(src, spot, k, (device, front)))
         if whole_pieces:
             dst[here] = src[...]
         else:
@@ -171,13 +172,11 @@
     def gather_xz(src, dst, slot, other_x):
         k, k_other = begin(), begin()
 
-        def step(i, _):
-            there, device = at_z(NZ, i)
+        def both(there, device):
             send(src, dst.at[slot, z], k_other, (other_x * NZ + there, front))
-            send(src, dst.at[slot, z], k, device)
-            return 0
-
-        lax.fori_loop(0, NZ - 1, step, 0)
+            send(src, dst.at[slot, z], k, (device, front))
+
+        each_z(NZ, both)
         send(src, dst.at[slot, z], k_other, (other_x * NZ + z, front))
         dst[slot, z] = src[...]
         sent.append((dst.at[0, pl.ds(0, NZ - 1)], k))
@@ -289,8 +288,7 @@
 
     greet((x * NZ + (z + 4) % NZ, front))
     greet((x * NZ + (z + 12) % NZ, front))
-    for i in range(3):
-        greet(at_z(4, i)[1])
+    each_z(4, lambda there, device: greet((device, front)))
     for d in (1, 2, 3):
         greet(at_x(d)[1])
         greet(at_y(d)[1])

time: 227 us -> 227 us (level)
  no operation moved by 1% of the time
where the time goes in v4:
time: 227 us; the launch traced here: 226 us
  Pallas kernels  222 us (98%)
  local copies, waits for them, and re-layouts  3.73 us (2%)
    pallas_call x1, Pallas kernels, per_device(): pl.pallas_call(kernel, out_shape=tuple((jax.ShapeDtypeStruct((1, 1, w, 12...  222 us

profile of v4, /device:TPU:1, one launch (start us, length us, event | category | flops | bytes accessed | tf_op | source)
XLA Modules:
  0.0 226.3 jit_solution(5828520987447924855)
XLA Ops:
  0.6 221.9 %solve.1 = (f32[1,1,6,128]{3,2,1,0:T(8,128)}, f32[1,1,12,128]{3,2,1,0:T(8,128)}, f32[1,1,24,128]{3,2,1,0:T(8,128)}, f32[1,1,48,128]{3,2,1,0:T(8,128)}, f32[1,1,96,128]{3,2,1,0:T(8,128)}) custom-call(s32[8,1,30]{2,1,0:T(1,128)} %bitcast.8, f32[1,6,1,128]{3,2,1,0:T(1,128)} %bitcast.9, f32[1,12,1,128]{3,2,1,0:T(1,128)} %bitcast.7, f32[1,1,24,128]{3,2,1,0:T(8,128)} %refs_2_.1, ...), custom_call_target="tpu_custom_call" | custom-call | flops 1200000000 | bytes 3000000 | tf_op jit(solution)/shard_map/solve/pallas_call | solution.py:469
  222.6 0.0 copy-start.3
  222.6 0.0 copy-start.2
  222.6 0.0 copy-start.1
  222.6 0.0 copy-start
  222.6 1.3 copy.20
  223.9 0.0 copy-done.3
  223.9 0.6 copy.21
  224.5 0.0 copy-done.2
  224.5 0.6 copy.25
  225.1 0.0 copy-done.1
  225.1 0.6 copy.26
  225.7 0.0 copy-done
  225.7 0.6 copy.27
Async XLA Ops:
  222.6 1.3 copy-start.3
  222.6 1.9 copy-start.2
  222.6 2.5 %copy-start.1 = (f32[1,1,48,128]{3,2,1,0:T(8,128)S(1)}, f32[1,1,48,128]{3,2,1,0:T(8,128)}, u32[]{:S(2)}) copy-start(f32[1,1,48,128]{3,2,1,0:T(8,128)} %get-tuple-element.18) | copy-start | bytes 73732
  222.6 3.1 %copy-start = (f32[1,1,96,128]{3,2,1,0:T(8,128)S(1)}, f32[1,1,96,128]{3,2,1,0:T(8,128)}, u32[]{:S(2)}) copy-start(f32[1,1,96,128]{3,2,1,0:T(8,128)} %get-tuple-element.19) | copy-start | bytes 147460

commit v5 on v4

--- a/solution.py
+++ b/solution.py
@@ -39,7 +39,7 @@
         SCRATCH[f"{_way}p{_l}"] = (2 * _h, 128)
         SCRATCH[f"{_way}c{_l}"] = (_h, 128)
         SCRATCH[f"{_way}h{_l}"] = (_h, 128)
-        if _l >= 3:
+        if _l >= 4:
             SCRATCH[f"{_way}r{_l}"] = (4, _h // 4, 128)
             SCRATCH[f"{_way}q{_l}"] = (_h // 4, 128)
             SCRATCH[f"{_way}g{_l}"] = (_h, 128)
@@ -219,7 +219,7 @@
         done = to_one(term.at[rows_of(1 - core, h)], from_core, core_mate)
         done()
         half[...] = term[rows_of(core, h), :] + from_core[...]
-        if level >= 3:
+        if level >= 4:
             q = h // 4
             piece = v[f"{way}q{level}"]
             done = to_y(lambda other: half.at[rows_of(other, q)], received.at[y], received.at[pl.ds(0, 3)])

time: 227 us -> 226 us (level)
  no operation moved by 1% of the time
where the time goes in v5:
time: 226 us
  Pallas kernels  222 us (98%)
  local copies, waits for them, and re-layouts  3.73 us (2%)
    pallas_call x1, Pallas kernels, per_device(): pl.pallas_call(kernel, out_shape=tuple((jax.ShapeDtypeStruct((1, 1, w, 12...  222 us

profile of v5, /device:TPU:1, one launch (start us, length us, event | category | flops | bytes accessed | tf_op | source)
XLA Modules:
  0.0 226.0 jit_solution(15367340501174133824)
XLA Ops:
  0.6 221.6 %solve.1 = (f32[1,1,6,128]{3,2,1,0:T(8,128)}, f32[1,1,12,128]{3,2,1,0:T(8,128)}, f32[1,1,24,128]{3,2,1,0:T(8,128)}, f32[1,1,48,128]{3,2,1,0:T(8,128)}, f32[1,1,96,128]{3,2,1,0:T(8,128)}) custom-call(s32[8,1,30]{2,1,0:T(1,128)} %bitcast.8, f32[1,6,1,128]{3,2,1,0:T(1,128)} %bitcast.9, f32[1,12,1,128]{3,2,1,0:T(1,128)} %bitcast.7, f32[1,1,24,128]{3,2,1,0:T(8,128)} %refs_2_.1, ...), custom_call_target="tpu_custom_call" | custom-call | flops 1200000000 | bytes 3000000 | tf_op jit(solution)/shard_map/solve/pallas_call | solution.py:469
  222.2 0.0 copy-start.3
  222.2 0.0 copy-start.2
  222.3 0.0 copy-start.1
  222.3 0.0 copy-start
  222.3 1.3 copy.20
  223.6 0.0 copy-done.3
  223.6 0.6 copy.21
  224.2 0.0 copy-done.2
  224.2 0.6 copy.25
  224.8 0.0 copy-done.1
  224.8 0.6 copy.26
  225.4 0.0 copy-done
  225.4 0.6 copy.27
Async XLA Ops:
  222.2 1.3 copy-start.3
  222.2 1.9 copy-start.2
  222.3 2.5 %copy-start.1 = (f32[1,1,48,128]{3,2,1,0:T(8,128)S(1)}, f32[1,1,48,128]{3,2,1,0:T(8,128)}, u32[]{:S(2)}) copy-start(f32[1,1,48,128]{3,2,1,0:T(8,128)} %get-tuple-element.18) | copy-start | bytes 73732
  222.3 3.1 %copy-start = (f32[1,1,96,128]{3,2,1,0:T(8,128)S(1)}, f32[1,1,96,128]{3,2,1,0:T(8,128)}, u32[]{:S(2)}) copy-start(f32[1,1,96,128]{3,2,1,0:T(8,128)} %get-tuple-element.19) | copy-start | bytes 147460
